TPU v7x, 512 devices: a whole 4x8x8 slice. The times are simulated.
512 devices in a mesh: lib: 16 (over x, y_hi, core), dom: 32 (over y_lo, z).
Axes of the slice: x: 4, y: 8 (y_hi: 2, y_lo: 4; y = y_hi * 4 + y_lo), z: 8, core: 2. Of those that a mesh axis runs over, the one named last changes fastest.
Arguments:
- images: bfloat16 [12288, 2, 9216], P(('lib', 'dom')), may hold values from -6 to 6
- classes: int32 [12288], P(('lib', 'dom')), may hold values from 0 to 7
- precision: float32 [12288], P(('lib', 'dom')), may hold values from 0.01 to 0.1
- counts: int32 [512], P(('lib', 'dom')), may hold values from 12 to 24, as said below
- shifts: int32 [9, 2], replicated, may hold values from -3 to 3
- ctf_table: float32 [8, 9216], replicated, may hold values from -1 to 1
- projections: bfloat16 [32, 2, 9216], P('lib'), may hold values from -1.71 to 1.71
Outputs:
- accum: float32 [32, 2, 9216], P('lib', None, 'dom')
- log_norm: float32 [12288], P(('lib', 'dom'))
Inputs may be any that keep to these rules, and one draw needn't show every extreme that they name: `counts`: each device has between 12 and 24 live slots, the first ones; some device has all 24 live.
All inputs are finite; a program needn't handle non-finite values.
Results may differ from a plain program's by a relative error of at most 0.0049.
Values may be sent and summed in bfloat16 or wider, within the bound.
A program may use at most 128 MiB of HBM per device.

v0:
```python
import jax
import jax.numpy as jnp
from jax import lax
from jax.sharding import PartitionSpec as P

FREQ = 96
SHIFTS = 9


def phase_tables(shifts, half):
    index = jnp.arange(half, dtype=jnp.int32)
    freq_x = (index % FREQ).astype(jnp.float32)
    freq_y = (index // FREQ - FREQ // 2).astype(jnp.float32)
    step_x = shifts[:, 0].astype(jnp.float32)[:, None]
    step_y = shifts[:, 1].astype(jnp.float32)[:, None]
    angle = 2.0 * jnp.pi / (2.0 * FREQ) * (step_x * freq_x[None, :] + step_y * freq_y[None, :])
    return (jnp.cos(angle), jnp.sin(angle))


def group_reduce(rows_fn, lib_rows):
    return lax.psum_scatter(
        rows_fn(jnp.int32(0), lax.axis_size("lib") * lib_rows),
        "lib",
        scatter_dimension=0,
        tiled=True,
    )


def body(images, classes, precision, counts, shifts, ctf_table, projections):
    slots = images.shape[0]
    half = images.shape[2]
    lib_rows = projections.shape[0]
    n_lib = lax.axis_size("lib")
    poses = lib_rows * n_lib
    cosine, sine = phase_tables(shifts, half)
    library = lax.all_gather(projections, "lib", axis=0, tiled=True)
    flat_lib = library.reshape(poses, 2 * half)
    lib_f = library.astype(jnp.float32)
    pose_power = lib_f[:, 0, :] ** 2 + lib_f[:, 1, :] ** 2
    power = lax.dot_general(
        ctf_table * ctf_table, pose_power, (((1,), (1,)), ((), ())), precision=lax.Precision.HIGHEST
    )
    onehot = (classes[:, None] == jnp.arange(ctf_table.shape[0], dtype=jnp.int32)[None, :]).astype(
        jnp.float32
    )
    ctf_rows = jnp.dot(onehot, ctf_table, precision=lax.Precision.HIGHEST)
    real_part = images[:, 0, :].astype(jnp.float32) * ctf_rows
    imag_part = images[:, 1, :].astype(jnp.float32) * ctf_rows
    re_s = real_part[:, None, :] * cosine[None] + imag_part[:, None, :] * sine[None]
    im_s = imag_part[:, None, :] * cosine[None] - real_part[:, None, :] * sine[None]
    shifted = (
        jnp.concatenate([re_s, im_s], axis=2).astype(jnp.bfloat16).reshape(slots * SHIFTS, 2 * half)
    )
    cross = lax.dot_general(
        shifted, flat_lib, (((1,), (1,)), ((), ())), preferred_element_type=jnp.float32
    )
    cross = cross.reshape(slots, SHIFTS, poses)
    class_power = jnp.dot(onehot, power, precision=lax.Precision.HIGHEST)
    score = precision[:, None, None] * (cross - 0.5 * class_power[:, None, :])
    live = jnp.arange(slots, dtype=jnp.int32) < counts[0]
    top = jnp.max(score, axis=(1, 2))
    log_norm = top + jnp.log(jnp.sum(jnp.exp(score - top[:, None, None]), axis=(1, 2)))
    weight = jnp.exp(score - log_norm[:, None, None]) * live[:, None, None].astype(jnp.float32)
    weight = weight.astype(jnp.bfloat16).reshape(slots * SHIFTS, poses)
    re_b = real_part[:, None, :] * cosine[None] - imag_part[:, None, :] * sine[None]
    im_b = imag_part[:, None, :] * cosine[None] + real_part[:, None, :] * sine[None]
    back = (
        jnp.concatenate([re_b, im_b], axis=2).astype(jnp.bfloat16).reshape(slots * SHIFTS, 2 * half)
    )

    def partial_rows(start, count):
        product = lax.dot_general(
            weight, back, (((0,), (0,)), ((), ())), preferred_element_type=jnp.float32
        )
        return product.reshape(count, 2, half)

    summed = group_reduce(partial_rows, lib_rows)
    accum = lax.psum_scatter(summed, "dom", scatter_dimension=2, tiled=True)
    return (accum, jnp.where(live, log_norm, jnp.zeros_like(log_norm)))


def solution(mesh):
    placed = (
        P(("lib", "dom"), None, None),
        P(("lib", "dom")),
        P(("lib", "dom")),
        P(("lib", "dom")),
        P(),
        P(),
        P("lib", None, None),
    )
    return jax.shard_map(
        body,
        mesh=mesh,
        in_specs=placed,
        out_specs=(P("lib", None, "dom"), P(("lib", "dom"))),
        check_vma=False,
    )
```

profile of v0, /device:TPU:4, one launch (start us, length us, event | category | flops | bytes accessed | tf_op | source)
XLA Modules:
  0.0 501.3 jit_solution(8494589481013526242)
XLA Ops:
  7.2 0.0 copy-start.1
  7.2 0.0 copy-start.2
  7.2 0.0 all-gather.2.cloned.1.call-start
  7.2 0.7 all-gather.2.cloned.1.call-update
  7.9 0.0 all-reduce.3.cloned.1.call-start
  8.0 0.8 convert_bitcast_fusion.1
  8.8 3.0 fusion.37
  12.4 2.2 fusion.22
  14.6 0.0 copy-done.1
  14.6 0.0 copy-done.2
  14.6 0.8 convert_multiply_fusion.1
  15.4 6.4 %fusion = (bf16[24,9,9216]{2,0,1:T(8,128)(2,1)}, bf16[24,9,9216]{2,0,1:T(8,128)(2,1)}, bf16[24,9,9216]{2,0,1:T(8,128)(2,1)S(1)}, bf16[24,9,9216]{2,0,1:T(8,128)(2,1)}) fusion(f32[9,9216]{1,0:T(8,128)S(1)} %get-tuple-element.19, f32[24,9216]{1,0:T(8,128)S(1)} %get-tuple-element.15, f32[9,9216]{1,0:T(8,128)S(1)} %get-tuple-element.18, ...), kind=kLoop, calls=%fused_computation.4 | loop fusion | flops 23887872 | bytes 18358272 | tf_op jit(solution)/shard_map/convert.6
  21.8 5.5 %copy.27 = bf16[24,9,9216]{2,1,0:T(8,128)(2,1)} copy(bf16[24,9,9216]{2,0,1:T(8,128)(2,1)S(1)} %get-tuple-element.12) | data formatting | bytes 7962624 | tf_op jit(solution)/shard_map/convert.4
  27.3 6.7 %add.64 = bf16[216,9216]{1,0:T(8,128)(2,1)} reshape(bf16[24,9,9216]{2,1,0:T(8,128)(2,1)} %copy.27) | data formatting | bytes 7962624 | tf_op jit(solution)/shard_map/add | solution.py:66
  34.0 7.6 %copy.26 = bf16[24,9,9216]{2,1,0:T(8,128)(2,1)} copy(bf16[24,9,9216]{2,0,1:T(8,128)(2,1)} %get-tuple-element.13) | data formatting | bytes 7962624 | tf_op jit(solution)/shard_map/convert.5
  41.6 6.7 %sub.54 = bf16[216,9216]{1,0:T(8,128)(2,1)} reshape(bf16[24,9,9216]{2,1,0:T(8,128)(2,1)} %copy.26) | data formatting | bytes 7962624 | tf_op jit(solution)/shard_map/sub | solution.py:65
  48.2 7.0 %pad_maximum_fusion = bf16[216,18432]{1,0:T(8,128)(2,1)} fusion(bf16[216,9216]{1,0:T(8,128)(2,1)} %add.64, bf16[216,9216]{1,0:T(8,128)(2,1)} %sub.54), kind=kLoop, calls=%fused_computation.15 | loop fusion | flops 15925248 | bytes 15925248 | tf_op jit(solution)/shard_map/concatenate | solution.py:68
  55.2 0.0 copy-start.3
  55.2 20.8 %all-gather.2.cloned.1.call-done = bf16[32,2,9216]{2,1,0:T(2,128)(2,1)} async-done(((bf16[2,2,9216]{2,1,0:T(2,128)(2,1)}), bf16[32,2,9216]{2,1,0:T(2,128)(2,1)}) %all-gather.2.cloned.1.call-update) | async-done | bytes 1179664 | tf_op jit(solution)/shard_map/all_gather | solution.py:36
  76.0 0.0 copy-start
  76.0 1.6 copy_convert_fusion
  77.6 1.0 fusion.13
  78.6 0.2 convolution_multiply_fusion
  78.9 0.0 copy-done
  78.9 1.0 reshape.207
  79.9 0.0 copy-done.3
  79.9 5.7 %fusion.38 = (f32[24]{0:T(128)S(1)}, f32[24,9,32]{2,0,1:T(8,128)S(1)}) fusion(f32[24,32]{1,0:T(8,128)S(1)} %convolution_multiply_fusion, bf16[32,18432,1]{1,0,2:T(8,128)(2,1)S(1)} %reshape.207, bf16[24,9,9216]{2,0,1:T(8,128)(2,1)} %get-tuple-element.11, bf16[24,9,9216]{2,0,1:T(8,128)(2,1)} %get-tuple-element.10, f32[24]{0:T(128)S(1)} %copy-done.3), kind=kOutput, calls=%fused_computation.61 | convolution fusion | flops 270749920 | bytes 9173184 | tf_op jit(solution)/shard_map/dot_general | solution.py:54
  85.6 0.2 exponential_reduce_fusion
  85.8 0.5 compare_select_fusion
  86.4 0.1 multiply_convert_fusion
  86.5 6.5 %fusion.4 = f32[32,2,9216]{2,0,1:T(8,128)} fusion(bf16[27,2,8,9216]{3,2,1,0:T(8,128)(2,1)} %bitcast.36, bf16[216,32]{1,0:T(8,128)(2,1)S(1)} %reshape.204), kind=kOutput, calls=%fused_computation.8 | convolution fusion | flops 254803968 | bytes 10335744 | tf_op jit(solution)/shard_map/dot_general | solution.py:72
  93.0 0.0 all-reduce.3.cloned.1.call-update
  93.0 0.0 reduce-scatter.5.cloned.1.call-start
  93.1 1.3 dynamic-slice
  95.0 200.2 %all-reduce.3.cloned.1.call-done = f32[32,2,9216]{2,0,1:T(8,128)} async-done(((f32[32,2,9216]{2,0,1:T(8,128)}), f32[32,2,9216]{2,0,1:T(8,128)}) %all-reduce.3.cloned.1.call-update) | async-done | bytes 2359312
  295.2 1.1 constant_dynamic-slice_fusion
  296.3 8.9 %copy.35 = f32[2,2,9216]{0,1,2:T(2,128)} copy(f32[2,2,9216]{2,0,1:T(2,128)S(1)} %constant_dynamic-slice_fusion) | data formatting | bytes 294912
  305.2 9.9 %reshape.212 = f32[9216,4]{1,0:T(8,128)} reshape(f32[9216,2,2]{2,1,0:T(2,128)} %bitcast.35) | data formatting | bytes 294912
  315.1 0.0 reduce-scatter.5.cloned.1.call-update
  315.1 177.7 %reduce-scatter.5.cloned.1.call-done = f32[288,4]{1,0:T(8,128)} async-done(((f32[9216,4]{1,0:T(8,128)}), f32[288,4]{1,0:T(8,128)}) %reduce-scatter.5.cloned.1.call-update) | async-done | bytes 4624
  492.9 1.1 reshape.213
  494.0 0.8 copy.30
  (4 shorter events, 0.1 us)
Async XLA Ops:
  7.2 7.4 %copy-start.1 = (f32[8,9216]{1,0:T(8,128)S(1)}, f32[8,9216]{1,0:T(8,128)}, u32[]{:S(2)}) copy-start(f32[8,9216]{1,0:T(8,128)} %param.12) | copy-start | bytes 884740
  7.2 7.4 %copy-start.2 = (s32[24]{0:T(128)S(1)}, s32[24]{0:T(128)}, u32[]{:S(2)}) copy-start(s32[24]{0:T(128)} %param.8) | copy-start | bytes 292
  7.2 68.8 %all-gather.2.cloned.1.call-start = ((), (), s32[]{:S(2)}) async-start(), calls=%async_computation.1 | async-start | bytes 1253376 | tf_op jit(solution)/shard_map/all_gather | solution.py:36
  7.9 287.3 %all-reduce.3.cloned.1.call-start = ((), (), s32[]{:S(2)}) async-start(), calls=%async_computation.3 | async-start | bytes 4718592
  55.2 24.7 %copy-start.3 = (f32[24]{0:T(128)S(1)}, f32[24]{0:T(128)}, u32[]{:S(2)}) copy-start(f32[24]{0:T(128)} %param.9) | copy-start | bytes 292
  76.0 2.8 copy-start
  93.0 399.8 %reduce-scatter.5.cloned.1.call-start = ((), (), s32[]{:S(2)}) async-start(), calls=%async_computation.2 | async-start | bytes 4866048
Sparse Core Ops, SparseCore 0:
  11.3 64.6 all-gather.1
  93.2 201.9 all-reduce.2
  315.3 177.5 reduce-scatter.4
where the time goes:
time: 502 us; the launch traced here: 501 us
  waiting for transfers between devices  399 us (79%)
  local copies, waits for them, and re-layouts  53.6 us (11%)
  other arithmetic  18.8 us (4%)
  between operations  15.2 us (3%)
  matrix products  14.2 us (3%)
    unnamed x5, waiting for transfers between devices  379 us
    unnamed x14, local copies, waits for them, and re-layouts  23.1 us
    all_gather x1, waiting for transfers between devices, body(): library = lax.all_gather(projections, 'lib', axis=0, tiled=True)  20.8 us
    another operation x2, local copies, waits for them, and re-layouts  13.1 us
  transfers between devices with their start and end apart: 3, of which 3 were waited for; matrix products, arithmetic and copies ran while one was open for 10% of the time, Pallas kernels for 0%

commit v1 on v0

v1 whole, which is shorter than its diff:
```python
import functools

import jax
import jax.numpy as jnp
import numpy as np
from jax import lax
from jax.experimental import pallas as pl
from jax.experimental.pallas import tpu as pltpu
from jax.sharding import PartitionSpec as P

FREQ = 96
SHIFTS = 9
HALF = 9216
CLASSES = 8
CAP = 24
POSES = 32
TILES = 72
RAW = 2 * TILES
WIDE = 2 * HALF
ROWS = 224
BLOCK = 2 * RAW + 16
STEP = 2.0 * np.pi / (2.0 * FREQ)
UNIT = 80
CHUNKS = ((0, 12), (12, 6))
MESH = pl.DeviceIdType.MESH
F32 = jnp.float32
BF16 = jnp.bfloat16


def place():
    lib = lax.axis_index("lib")
    dom = lax.axis_index("dom")
    return lib // 4, (lib // 2) % 2, dom // 8, dom % 8, lib % 2


def device(x, y, z, core):
    return ((x * 2 + y // 4) * 2 + core, (y % 4) * 8 + z)


def kernel(
    classes_ref, precision_ref, counts_ref, shifts_ref, img_hbm, ctf_hbm, proj_hbm,
    accum_ref, norm_ref,
    img, ctf, raw, crow, shifted, back, lib_in, lib_f, lib_b, own_f,
    acc, core_out, core_in, x_out, x_in, y_own, y_out, y_in, z_own, z_out, z_in,
    local_sem, send_sem, recv_sem,
):
    x, yh, yl, z, core = place()
    y = yh * 4 + yl
    me = (x * 2 + yh) * 2 + core
    right, left, across = (x + 1) % 4, (x + 3) % 4, (x + 2) % 4
    mate = 1 - core
    slots = iter(range(100))

    def slot_of(px, pyh, pcore):
        return (px * 2 + pyh) * 2 + pcore

    def remote(src, dst, target):
        k = next(slots)
        return pltpu.make_async_remote_copy(
            src_ref=src, dst_ref=dst, send_sem=send_sem.at[k], recv_sem=recv_sem.at[k],
            device_id=target, device_id_type=MESH,
        )

    img_copy = pltpu.make_async_copy(img_hbm, img, local_sem.at[0])
    ctf_copy = pltpu.make_async_copy(ctf_hbm, ctf, local_sem.at[1])
    own_copy = pltpu.make_async_copy(proj_hbm, lib_in.at[me, pl.ds(0, 2 * RAW)], local_sem.at[2])
    own_copy.start()
    ctf_copy.start()
    img_copy.start()
    partners = [device((x + d) % 4, y, z, core) for d in range(1, 4)]
    partners += [device(x, (y + d) % 8, z, core) for d in range(1, 8)]
    partners += [device(x, y, (z + d) % 8, core) for d in range(1, 8)]
    partners += [device(x, y, z, mate)]
    barrier = pltpu.get_barrier_semaphore()
    for partner in partners:
        pl.semaphore_signal(barrier, inc=1, device_id=partner, device_id_type=MESH)

    own_copy.wait()
    ctf_copy.wait()
    own_f[...] = lib_in[me, pl.ds(0, 2 * RAW), :].astype(F32)
    lane = lax.broadcasted_iota(jnp.int32, (8, 128), 1)
    tile = jnp.zeros((8, 128), F32)
    for p in range(2):
        re = own_f[pl.ds(p * RAW, TILES, stride=2), :]
        im = own_f[pl.ds(p * RAW + 1, TILES, stride=2), :]
        both = re * re + im * im
        total = jnp.zeros((8, 128), F32)
        for t in range(TILES):
            c = ctf[:, t * 128:(t + 1) * 128]
            total = total + (c * c) * both[t:t + 1, :]
        power = jnp.sum(total, axis=1, keepdims=True)
        hi = power.astype(BF16).astype(F32)
        mid = (power - hi).astype(BF16).astype(F32)
        low = power - hi - mid
        column = core * 16 + p * 8 + x * 2 + yh
        for k, part in enumerate((hi, mid, low)):
            tile = tile + jnp.where(lane == column + 32 * k, part, 0.0)
    lib_in[me, pl.ds(2 * RAW, 16), :] = jnp.concatenate([tile, jnp.zeros((8, 128), F32)], axis=0).astype(BF16)

    pl.semaphore_wait(barrier, len(partners))

    sent = []

    def block_to(slot, target, rows=None):
        view = lib_in.at[slot] if rows is None else lib_in.at[slot, pl.ds(*rows)]
        return remote(view, view, target)

    FIRST, SECOND = (0, 160), (160, BLOCK - 160)
    sides = (device(right, y, z, core), device(left, y, z, core))
    pair = device(x, y, z, mate)
    own_sends = [block_to(me, sides[0]), block_to(me, sides[1]), block_to(me, pair)]
    other = slot_of(x, 1 - yh, core)
    up, down = device(x, (y + 1) % 8, z, core), device(x, (y + 7) % 8, z, core)
    cross_down = block_to(me, down)
    cross_up = block_to(me, up)
    inner_up = block_to(other, up)
    inner_down = block_to(other, down)

    @pl.when(yl == 0)
    def _():
        cross_down.start()

    @pl.when(yl == 3)
    def _():
        cross_up.start()

    for copy in own_sends:
        copy.start()
    sent += own_sends

    def column_of(row):
        r = lax.broadcasted_iota(jnp.int32, (CAP, CAP), 0)
        c = lax.broadcasted_iota(jnp.int32, (CAP, CAP), 1)
        return jnp.sum(jnp.where(r == c, jnp.broadcast_to(row, (CAP, CAP)), 0.0), axis=1, keepdims=True)

    klass = column_of(classes_ref[...].astype(F32))
    prec = column_of(precision_ref[...])
    kinds = lax.broadcasted_iota(jnp.int32, (CAP, CLASSES), 1).astype(F32)
    onehot = (klass == kinds).astype(F32)
    pick = jnp.concatenate([onehot, onehot, onehot], axis=1).astype(BF16)
    for k in range(9):
        cols = slice(k * 1024, (k + 1) * 1024)
        c = ctf[:, cols]
        hi = c.astype(BF16).astype(F32)
        mid = (c - hi).astype(BF16).astype(F32)
        low = c - hi - mid
        parts = jnp.concatenate([hi, mid, low], axis=0).astype(BF16)
        crow[:, cols] = jnp.dot(pick, parts, preferred_element_type=F32)

    row16 = lax.broadcasted_iota(jnp.int32, (16, 128), 0)
    step_x = jnp.zeros((16, 128), F32)
    step_y = jnp.zeros((16, 128), F32)
    for s in range(SHIFTS):
        step_x = jnp.where(row16 == s, shifts_ref[s, 0].astype(F32), step_x)
        step_y = jnp.where(row16 == s, shifts_ref[s, 1].astype(F32), step_y)
    fine = []
    lanes = lax.broadcasted_iota(jnp.int32, (16, 128), 1)
    for u in range(3):
        j = lanes + u * 128
        dy = (j >= 96).astype(jnp.int32) + (j >= 192).astype(jnp.int32) + (j >= 288).astype(jnp.int32)
        kx = j - 96 * dy
        angle = STEP * (step_x * kx.astype(F32) + step_y * dy.astype(F32))
        fine.append((jnp.cos(angle), jnp.sin(angle)))
    start = STEP * (step_y * float(-(FREQ // 2)))
    turn = STEP * (step_y * 4.0)
    turn_c, turn_s = jnp.cos(turn), jnp.sin(turn)

    img_copy.wait()

    def widen(n, carry):
        rows = pl.ds(pl.multiple_of(n * RAW, 16), RAW)
        raw[rows, :] = img[rows, :].astype(F32)
        return carry

    lax.fori_loop(0, CAP, widen, 0)
    zeros8 = jnp.zeros((8, 128), F32)

    def shift_tiles(q, carry):
        base_c, base_s = carry
        for u in range(3):
            t = 3 * q + u
            fc, fs = fine[u]
            cosine = fc * base_c - fs * base_s
            sine = fs * base_c + fc * base_s
            c_tile = crow[:, pl.ds(pl.multiple_of(t * 128, 128), 128)]
            real, imag = [], []
            for g in range(3):
                c = c_tile[8 * g:8 * g + 8, :]
                real.append(raw[pl.ds(g * 8 * RAW + 2 * t, 8, stride=RAW), :] * c)
                imag.append(raw[pl.ds(g * 8 * RAW + 2 * t + 1, 8, stride=RAW), :] * c)
            re_s, im_s, re_b, im_b = [], [], [], []
            for s in range(SHIFTS):
                cs = jnp.broadcast_to(cosine[s:s + 1, :], (8, 128))
                sn = jnp.broadcast_to(sine[s:s + 1, :], (8, 128))
                for g in range(3):
                    ac, bs = real[g] * cs, imag[g] * sn
                    bc, as_ = imag[g] * cs, real[g] * sn
                    re_s.append(ac + bs)
                    im_s.append(bc - as_)
                    re_b.append(ac - bs)
                    im_b.append(bc + as_)
            for dst, parts in ((shifted, (re_s, im_s)), (back, (re_b, im_b))):
                for k, part in enumerate(parts):
                    cols = pl.ds(pl.multiple_of(t * 256 + k * 128, 128), 128)
                    dst[:, cols] = jnp.concatenate(part + [zeros8], axis=0).astype(BF16)
        return base_c * turn_c - base_s * turn_s, base_s * turn_c + base_c * turn_s

    phase = (jnp.cos(start), jnp.sin(start))
    phase = lax.fori_loop(0, 8, shift_tiles, phase)

    @pl.when(yl == 0)
    def _():
        cross_up.wait_recv()
        inner_up.start()

    @pl.when(yl == 3)
    def _():
        cross_down.wait_recv()
        inner_down.start()

    @pl.when(yl == 1)
    def _():
        inner_up.wait_recv()

    @pl.when(yl == 2)
    def _():
        inner_down.wait_recv()

    other_sends = [block_to(other, sides[0]), block_to(other, sides[1]), block_to(other, pair)]
    for copy in other_sends:
        copy.start()
    sent += other_sends
    phase = lax.fori_loop(8, 16, shift_tiles, phase)

    def hand_on(h, sends):
        from_left, from_right = slot_of(left, h, core), slot_of(right, h, core)
        copies = [block_to(from_left, sides[0], FIRST), block_to(from_left, pair)]
        sends[0].wait_recv()
        for copy in copies:
            copy.start()
        more = [block_to(from_right, sides[1], SECOND), block_to(from_right, pair)]
        sends[1].wait_recv()
        for copy in more:
            copy.start()
        return copies + more

    def finish(h, copies):
        copies[0].wait_recv()
        copies[2].wait_recv()
        copy = block_to(slot_of(across, h, core), pair)
        copy.start()
        return copy

    own_on = hand_on(yh, own_sends)
    sent += own_on
    phase = lax.fori_loop(16, 24, shift_tiles, phase)
    own_last = finish(yh, own_on)
    other_on = hand_on(1 - yh, other_sends)
    other_last = finish(1 - yh, other_on)
    sent += [own_last] + other_on + [other_last]
    for copy in (own_sends[2], other_sends[2], own_on[1], own_on[3], own_last, other_on[1], other_on[3], other_last):
        copy.wait_recv()

    def widen_lib(k, carry):
        lib_f[pl.ds(pl.multiple_of(k * 2 * RAW, 16), 2 * RAW), :] = lib_in[k, pl.ds(0, 2 * RAW), :].astype(F32)
        return carry

    lax.fori_loop(0, 16, widen_lib, 0)
    powers = jnp.zeros((8, 128), F32)
    for k in range(16):
        powers = powers + lib_in[k, pl.ds(2 * RAW, 16), :].astype(F32)[0:8, :]
    power = powers[:, 0:32] + powers[:, 32:64] + powers[:, 64:96]

    def gather_tiles(q, carry):
        for u in range(4):
            t = q * 4 + u
            halves = []
            for k in range(2):
                parts = [
                    lib_f[pl.ds(c * 2 * RAW + p * RAW + 2 * t + k, 8, stride=4 * RAW), :]
                    for c in range(2) for p in range(2)
                ]
                halves.append(jnp.concatenate(parts, axis=0))
            cols = pl.ds(pl.multiple_of(t * 256, 256), 256)
            lib_b[:, cols] = jnp.concatenate(halves, axis=1).astype(BF16)
        return carry

    lax.fori_loop(0, TILES // 4, gather_tiles, 0)

    def cross_part(q, total):
        cols = pl.ds(pl.multiple_of(q * 4608, 4608), 4608)
        return total + lax.dot_general(
            shifted[:, cols], lib_b[:, cols], (((1,), (1,)), ((), ())), preferred_element_type=F32
        )

    cross = lax.fori_loop(0, 4, cross_part, jnp.zeros((ROWS, POSES), F32))
    class_power = jnp.zeros((CAP, POSES), F32)
    for k in range(CLASSES):
        class_power = class_power + jnp.where(klass == float(k), power[k:k + 1, :], 0.0)
    scores = [prec * (cross[s * CAP:(s + 1) * CAP, :] - 0.5 * class_power) for s in range(SHIFTS)]
    top = scores[0]
    for s in range(1, SHIFTS):
        top = jnp.maximum(top, scores[s])
    top = jnp.max(top, axis=1, keepdims=True)
    mass = jnp.exp(scores[0] - top)
    for s in range(1, SHIFTS):
        mass = mass + jnp.exp(scores[s] - top)
    log_norm = top + jnp.log(jnp.sum(mass, axis=1, keepdims=True))
    live = lax.broadcasted_iota(jnp.int32, (CAP, 1), 0) < counts_ref[0]
    r24 = lax.broadcasted_iota(jnp.int32, (CAP, 128), 0)
    c24 = lax.broadcasted_iota(jnp.int32, (CAP, 128), 1)
    shown = jnp.where(live, log_norm, 0.0)
    norm_ref[...] = jnp.sum(jnp.where(r24 == c24, shown, 0.0), axis=0, keepdims=True)
    weights = [jnp.where(live, jnp.exp(score - log_norm), 0.0) for score in scores]
    weight = jnp.concatenate(weights + [jnp.zeros((8, POSES), F32)], axis=0).astype(BF16)
    unit = lax.broadcasted_iota(jnp.int32, (POSES, POSES), 0) == lax.broadcasted_iota(jnp.int32, (POSES, POSES), 1)
    weight_t = lax.dot_general(
        unit.astype(F32).astype(BF16), weight, (((1,), (1,)), ((), ())), preferred_element_type=F32
    ).astype(BF16)

    for c in range(2):
        for g in range(32):
            acc[pl.ds(c * 2560 + g * UNIT + 72, 8), :] = zeros8
    core_sends = []
    for first, count in CHUNKS:
        low, high = first * 4, 48 if first == 0 else UNIT

        def sum_quarter(quarter, carry):
            cols = pl.ds(pl.multiple_of((quarter * 18 + first) * 256, 256), count * 256)
            part = jnp.dot(weight_t, back[:, cols], preferred_element_type=F32)
            for c in range(2):
                for p in range(2):
                    r = c * 16 + p * 8
                    for k in range(2 * count):
                        row = c * 2560 + quarter * UNIT + (first * 2 + k) * 2 + p
                        acc[pl.ds(row, 8, stride=4 * UNIT), :] = part[r:r + 8, k * 128:(k + 1) * 128]
            for g in range(8):
                rows = pl.ds(pl.multiple_of(mate * 2560 + (g * 4 + quarter) * UNIT + low, 16), high - low)
                core_out[g, quarter, pl.ds(low, high - low), :] = acc[rows, :].astype(BF16)
            return carry

        lax.fori_loop(0, 4, sum_quarter, 0)
        rows = pl.ds(low, high - low)
        copy = remote(core_out.at[:, :, rows], core_in.at[:, :, rows], pair)
        copy.start()
        core_sends.append(copy)
    sent += core_sends

    x_sends = []
    for (first, count), core_copy in zip(CHUNKS, core_sends):
        low, high = first * 4, 48 if first == 0 else UNIT
        rows = pl.ds(low, high - low)
        core_copy.wait_recv()
        copies = []
        for d in (2, 1, 3):
            px = (x + d) % 4
            for h in range(2):
                for quarter in range(4):
                    at = pl.ds(pl.multiple_of(core * 2560 + ((px * 2 + h) * 4 + quarter) * UNIT + low, 16), high - low)
                    part = acc[at, :] + core_in[px * 2 + h, quarter, rows, :].astype(F32)
                    x_out[d - 1, h, quarter, rows, :] = part.astype(BF16)
            copy = remote(
                x_out.at[d - 1, :, :, rows], x_in.at[d - 1, :, :, rows], device(px, y, z, core)
            )
            copy.start()
            copies.append(copy)
        x_sends.append(copies)
        sent += copies

    y_sends = []
    for (first, count), copies in zip(CHUNKS, x_sends):
        low, high = first * 4, 48 if first == 0 else UNIT
        rows = pl.ds(low, high - low)
        for copy in copies:
            copy.wait_recv()
        for h in range(2):
            for quarter in range(4):
                at = pl.ds(pl.multiple_of(core * 2560 + ((x * 2 + h) * 4 + quarter) * UNIT + low, 16), high - low)
                part = acc[at, :] + core_in[x * 2 + h, quarter, rows, :].astype(F32)
                for d in range(3):
                    part = part + x_in[d, h, quarter, rows, :].astype(F32)
                y_own[h * 4 + quarter, rows, :] = part
                y_out[h * 4 + quarter, rows, :] = part.astype(BF16)
        copies = []
        for d in (4, 3, 5, 2, 6, 1, 7):
            py = (y + d) % 8
            copy = remote(y_out.at[py, rows], y_in.at[d - 1, rows], device(x, py, z, core))
            copy.start()
            copies.append(copy)
        y_sends.append(copies)
        sent += copies

    for (first, count), copies in zip(CHUNKS, y_sends):
        low, high = first * 4, 48 if first == 0 else UNIT
        rows = pl.ds(low, high - low)
        for copy in copies:
            copy.wait_recv()
        part = y_own[y, rows, :]
        for d in range(7):
            part = part + y_in[d, rows, :].astype(F32)
        z_own[rows, :] = part

    for k in range(8):
        first = 36 * (k // 4) + 8 * (k % 4)
        part = z_own[first:first + 16, :]
        y_own[k, pl.ds(0, 16), :] = part
        z_out[k] = part.astype(BF16)
    z_sends = []
    for d in (4, 3, 5, 2, 6, 1, 7):
        pz = (z + d) % 8
        copy = remote(z_out.at[pz], z_in.at[d - 1], device(x, y, pz, core))
        copy.start()
        z_sends.append(copy)
    sent += z_sends
    for copy in z_sends:
        copy.wait_recv()
    part = y_own[z, pl.ds(0, 16), :]
    for d in range(7):
        part = part + z_in[d].astype(F32)
    skip = (z % 4) * 32
    turned = pltpu.roll(part, (128 - skip) % 128, 1)
    keep = lax.broadcasted_iota(jnp.int32, (4, 128), 1) < 128 - skip
    for t in range(3):
        piece = turned[4 * t:4 * t + 4, :]
        if t < 2:
            piece = jnp.where(keep, piece, turned[4 * t + 4:4 * t + 8, :])
        width = 128 if t < 2 else 32
        for p in range(2):
            for c in range(2):
                accum_ref[p, c:c + 1, t * 128:t * 128 + width] = piece[c * 2 + p:c * 2 + p + 1, 0:width]

    for copy in sent:
        copy.wait_send()

    @pl.when(yl == 0)
    def _():
        cross_down.wait_send()
        inner_up.wait_send()

    @pl.when(yl == 3)
    def _():
        cross_up.wait_send()
        inner_down.wait_send()


def body(images, classes, precision, counts, shifts, ctf_table, projections):
    raw_img = images.reshape(CAP, 2, TILES, 128).transpose(0, 2, 1, 3).reshape(CAP * RAW, 128)
    raw_proj = projections.reshape(2, 2, TILES, 128).transpose(0, 2, 1, 3).reshape(2 * RAW, 128)
    vmem = pl.BlockSpec(memory_space=pltpu.VMEM)
    smem = pl.BlockSpec(memory_space=pltpu.SMEM)
    anywhere = pl.BlockSpec(memory_space=pl.ANY)
    accum, norm = pl.pallas_call(
        kernel,
        out_shape=(
            jax.ShapeDtypeStruct((2, 2, HALF // 32), F32),
            jax.ShapeDtypeStruct((1, 128), F32),
        ),
        in_specs=[vmem, vmem, smem, smem, anywhere, anywhere, anywhere],
        out_specs=(vmem, vmem),
        scratch_shapes=[
            pltpu.VMEM((CAP * RAW, 128), BF16),
            pltpu.VMEM((CLASSES, HALF), F32),
            pltpu.VMEM((CAP * RAW, 128), F32),
            pltpu.VMEM((CAP, HALF), F32),
            pltpu.VMEM((ROWS, WIDE), BF16),
            pltpu.VMEM((ROWS, WIDE), BF16),
            pltpu.VMEM((16, BLOCK, 128), BF16),
            pltpu.VMEM((32 * RAW, 128), F32),
            pltpu.VMEM((POSES, WIDE), BF16),
            pltpu.VMEM((2 * RAW, 128), F32),
            pltpu.VMEM((64 * UNIT, 128), F32),
            pltpu.VMEM((8, 4, UNIT, 128), BF16),
            pltpu.VMEM((8, 4, UNIT, 128), BF16),
            pltpu.VMEM((3, 2, 4, UNIT, 128), BF16),
            pltpu.VMEM((3, 2, 4, UNIT, 128), BF16),
            pltpu.VMEM((8, UNIT, 128), F32),
            pltpu.VMEM((8, UNIT, 128), BF16),
            pltpu.VMEM((7, UNIT, 128), BF16),
            pltpu.VMEM((UNIT, 128), F32),
            pltpu.VMEM((8, 16, 128), BF16),
            pltpu.VMEM((7, 16, 128), BF16),
            pltpu.SemaphoreType.DMA((3,)),
            pltpu.SemaphoreType.DMA((64,)),
            pltpu.SemaphoreType.DMA((64,)),
        ],
        compiler_params=pltpu.CompilerParams(
            collective_id=0, has_side_effects=True, vmem_limit_bytes=56 * 1024 * 1024
        ),
        name="expectation",
    )(classes.reshape(1, CAP), precision.reshape(1, CAP), counts, shifts, raw_img, ctf_table, raw_proj)
    return accum, norm.reshape(128)[:CAP]


def solution(mesh):
    placed = (
        P(("lib", "dom"), None, None),
        P(("lib", "dom")),
        P(("lib", "dom")),
        P(("lib", "dom")),
        P(),
        P(),
        P("lib", None, None),
    )
    return jax.shard_map(
        body,
        mesh=mesh,
        in_specs=placed,
        out_specs=(P("lib", None, "dom"), P(("lib", "dom"))),
        check_vma=False,
    )
```

time: 502 us -> 65.2 us (0.13)
  the two profiles are of different devices: /device:TPU:4 before, /device:TPU:1 now
where the time goes in v1:
time: 65.2 us; the launch traced here: 64.9 us
  Pallas kernels  59.8 us (92%)
  local copies, waits for them, and re-layouts  3.75 us (6%)
  between operations  1.3 us (2%)
    pallas_call x1, Pallas kernels, body(): pl.pallas_call(kernel, out_shape=(jax.ShapeDtypeStruct((2, 2, HALF // 32)...  59.8 us
    unnamed x6, local copies, waits for them, and re-layouts  3.24 us

profile of v1, /device:TPU:1, one launch (start us, length us, event | category | flops | bytes accessed | tf_op | source)
XLA Modules:
  0.0 64.9 jit_solution(6569041386840300453)
XLA Ops:
  1.3 0.0 copy-start
  1.3 0.7 %copy-done = s32[9,2]{0,1:T(2,128)S(1)} copy-done((s32[9,2]{0,1:T(2,128)S(1)}, s32[9,2]{0,1:T(2,128)}, u32[]{:S(2)}) %copy-start) | copy-done | bytes 96
  2.0 0.7 %copy.11.shifts_ref = s32[9,2]{1,0:T(8,128)} copy(s32[9,2]{0,1:T(2,128)S(1)} %copy-done) | data formatting | bytes 144 | tf_op args[4]
  2.6 59.8 %expectation.1 = (f32[2,2,288]{2,1,0:T(2,128)}, f32[1,128]{1,0:T(1,128)}) custom-call(s32[1,24]{1,0:T(1,128)} %bitcast.16, f32[1,24]{1,0:T(1,128)} %bitcast.17, s32[1]{0:T(128)S(6)} %copy.13.counts_ref, s32[9,2]{1,0:T(8,128)} %copy.11.shifts_ref, bf16[3456,128]{1,0:T(8,128)(2,1)} %bitcast.14, f32[8,9216]{1,0:T(8,128)} %ctf_hbm.1, bf16[288,128]{1,0:T(8,128)(2,1)} %bitcast.15), custom_call_target="tpu_custom_call" | custom-call | tf_op jit(solution)/shard_map/expectation/pallas_call | solution.py:452
  62.5 0.0 copy-start.1
  62.5 0.6 copy-done.1
  63.1 0.5 slice_bitcast_fusion
  63.6 1.3 %copy.14 = f32[2,2,288]{2,1,0:T(2,128)} copy(f32[2,2,288]{2,1,0:T(2,128)} %get-tuple-element.8) | data formatting | bytes 9216
Async XLA Ops:
  1.3 0.7 %copy-start = (s32[9,2]{0,1:T(2,128)S(1)}, s32[9,2]{0,1:T(2,128)}, u32[]{:S(2)}) copy-start(s32[9,2]{0,1:T(2,128)} %param.11) | copy-start | bytes 220
  62.5 0.6 copy-start.1

commit v2 on v0

v2 whole, which is shorter than its diff:
```python
import functools

import jax
import jax.numpy as jnp
import numpy as np
from jax import lax
from jax.experimental import pallas as pl
from jax.experimental.pallas import tpu as pltpu
from jax.sharding import PartitionSpec as P

FREQ = 96
SHIFTS = 9
HALF = 9216
CLASSES = 8
CAP = 24
POSES = 32
TILES = 72
RAW = 2 * TILES
WIDE = 2 * HALF
PAIR = 2 * CAP
ROWS = SHIFTS * PAIR
HALF_TILES = TILES // 2
BLOCK = HALF_TILES * 4
LIB_CHUNKS = ((0, 20), (20, 16))
STEP = 2.0 * np.pi / (2.0 * FREQ)
UNIT = 80
CHUNKS = ((0, 4, 0, 32), (4, 5, 32, 80))
MESH = pl.DeviceIdType.MESH
F32 = jnp.float32
BF16 = jnp.bfloat16


def place():
    lib = lax.axis_index("lib")
    dom = lax.axis_index("dom")
    return lib // 4, (lib // 2) % 2, dom // 8, dom % 8, lib % 2


def device(x, y, z, core):
    return ((x * 2 + y // 4) * 2 + core, (y % 4) * 8 + z)


def kernel(
    classes_hbm, precision_hbm, counts_hbm, shifts_hbm, img_hbm, ctf_hbm, proj_hbm,
    accum_ref, norm_ref,
    classes_v, precision_v, counts_v, shifts_v, proj,
    img, ctf, raw, crow, shifted, back, meta, own_f, own_r, own_b, lib_in, lib_f, lib_b, power_f,
    mine, theirs, acc, x_out, x_in, y_own, y_out, y_in, z_own, z_f, z_out, z_in,
    local_sem, send_sem, recv_sem,
):
    x, yh, yl, z, core = place()
    y = yh * 4 + yl
    me = (x * 2 + yh) * 2 + core
    mate = 1 - core
    pair = device(x, y, z, mate)
    far = (y + 4) % 8
    base = core * 9
    send_slots, recv_slots = iter(range(200)), iter(range(200))

    def remote(src, dst, target, recv=None):
        recv = next(recv_slots) if recv is None else recv
        return pltpu.make_async_remote_copy(
            src_ref=src, dst_ref=dst, send_sem=send_sem.at[next(send_slots)], recv_sem=recv_sem.at[recv],
            device_id=target, device_id_type=MESH,
        )

    def arrival(dst, recv):
        return pltpu.make_async_remote_copy(
            src_ref=dst, dst_ref=dst, send_sem=send_sem.at[0], recv_sem=recv_sem.at[recv],
            device_id=pair, device_id_type=MESH,
        )

    sources = [device((x + d) % 4, y, z, c) for d in (1, 2, 3) for c in (0, 1)]
    sources += [device(x, far, z, mate)]
    sources += [device(x, (y + d) % 8, z, core) for d in range(1, 8)]
    sources += [device(x, y, (z + d) % 8, z // 4) for d in range(1, 8)]
    barrier = pltpu.get_barrier_semaphore()
    pl.semaphore_signal(barrier, inc=1, device_id=pair, device_id_type=MESH)
    for source in sources:
        pl.semaphore_signal(barrier, inc=1, device_id=source, device_id_type=MESH)
    copies = [
        pltpu.make_async_copy(src, dst, local_sem.at[k])
        for k, (src, dst) in enumerate((
            (proj_hbm, proj), (classes_hbm, classes_v), (precision_hbm, precision_v), (counts_hbm, counts_v),
            (shifts_hbm, shifts_v), (ctf_hbm, ctf), (img_hbm, img.at[core]),
        ))
    ]
    for copy in copies:
        copy.start()

    copies[0].wait()
    own_f[...] = proj[...].astype(F32)
    for h in range(2):
        for q in range(4):
            for p in range(2):
                for c in range(2):
                    rows = own_f[pl.ds(p * RAW + 36 * q + 18 * h + c, 9, stride=2), :]
                    own_r[pl.ds(h * BLOCK + 36 * q + 2 * c + p, 9, stride=4), :] = rows
    own_b[0] = own_r[0:BLOCK, :].astype(BF16)
    own_b[1] = own_r[BLOCK:2 * BLOCK, :].astype(BF16)
    lib_in[me] = own_b[core]

    for copy in copies[1:4]:
        copy.wait()

    def column_of(row, size):
        r = lax.broadcasted_iota(jnp.int32, (size, row.shape[1]), 0)
        c = lax.broadcasted_iota(jnp.int32, (size, row.shape[1]), 1)
        return jnp.sum(jnp.where(r == c, jnp.broadcast_to(row, r.shape), 0.0), axis=1, keepdims=True)

    lane24 = lax.broadcasted_iota(jnp.int32, (CAP, 128), 1)
    alive = lax.broadcasted_iota(jnp.int32, (CAP, 1), 0) < counts_v[...]
    meta[core] = jnp.where(
        lane24 == 0, column_of(classes_v[...].astype(F32), CAP),
        jnp.where(lane24 == 1, column_of(precision_v[...], CAP), jnp.where(alive, 1.0, 0.0)),
    )
    pl.semaphore_wait(barrier, 15 + jnp.where(z // 4 == core, 6, 8))

    sent = []
    meta_copy = remote(meta.at[core], meta.at[core], pair)
    block_copy = remote(own_b.at[mate], lib_in.at[me], pair)
    img_copy = remote(img_hbm, img.at[core], pair)
    targets = [(x, far)] + [((x + d) % 4, y) for d in (1, 3, 2)]
    first_slots = []
    for first, count in LIB_CHUNKS:
        rows = pl.ds(first * 4, count * 4)
        slots = []
        for px, py in targets:
            pick = [next(recv_slots), next(recv_slots)]
            slots.append(pick)
            for h in range(2):
                copy = remote(
                    own_b.at[h, rows], lib_in.at[me, rows], device(px, py, z, h), pick[0] + core
                )
                copy.start()
                sent.append(copy)
        first_slots.append(slots)
    for copy in (meta_copy, block_copy, img_copy):
        copy.start()
        sent.append(copy)

    copies[4].wait()
    step = shifts_v[...].astype(F32)
    step_x = jnp.broadcast_to(column_of(step[0:1, :], 16), (16, 128))
    step_y = jnp.broadcast_to(column_of(step[1:2, :], 16), (16, 128))
    fine = []
    lanes = lax.broadcasted_iota(jnp.int32, (16, 128), 1)
    for u in range(3):
        j = lanes + u * 128
        dy = (j >= 96).astype(jnp.int32) + (j >= 192).astype(jnp.int32) + (j >= 288).astype(jnp.int32)
        kx = j - 96 * dy
        angle = STEP * (step_x * kx.astype(F32) + step_y * dy.astype(F32))
        fine.append((jnp.cos(angle), jnp.sin(angle)))
    start = STEP * (step_y * (12 * core - FREQ // 2).astype(F32))
    turn = STEP * (step_y * 4.0)
    leap = STEP * (step_y * 16.0)
    turn_c, turn_s, leap_c, leap_s = jnp.cos(turn), jnp.sin(turn), jnp.cos(leap), jnp.sin(leap)
    phase = (jnp.cos(start), jnp.sin(start))

    copies[5].wait()
    arrival(meta.at[mate], 0).wait_recv()
    both = jnp.concatenate([meta[0], meta[1]], axis=0)
    klass, prec, live = both[:, 0:1], both[:, 1:2], both[:, 2:3]
    kinds = lax.broadcasted_iota(jnp.int32, (PAIR, CLASSES), 1).astype(F32)
    onehot = (klass == kinds).astype(F32)
    pick = jnp.concatenate([onehot, onehot, onehot], axis=1).astype(BF16)
    for q in range(4):
        c = ctf[:, pl.ds(pl.multiple_of((18 * q + base) * 128, 128), 1152)]
        hi = c.astype(BF16).astype(F32)
        mid = (c - hi).astype(BF16).astype(F32)
        low = c - hi - mid
        parts = jnp.concatenate([hi, mid, low], axis=0).astype(BF16)
        crow[:, q * 1152:(q + 1) * 1152] = jnp.dot(pick, parts, preferred_element_type=F32)

    def widen(n, carry):
        for c in range(2):
            src = pl.ds(pl.multiple_of(n * RAW, 16), RAW)
            raw[pl.ds(pl.multiple_of((c * CAP + n) * RAW, 16), RAW), :] = img[c, src, :].astype(F32)
        return carry

    copies[6].wait()
    arrival(img.at[mate], 2).wait_recv()
    lax.fori_loop(0, CAP, widen, 0)

    def shift_tiles(i, carry):
        base_c, base_s = carry
        q, v = i // 3, i % 3
        for u in range(3):
            t = 18 * q + base + 3 * v + u
            tt = 3 * i + u
            fc, fs = fine[u]
            cosine = fc * base_c - fs * base_s
            sine = fs * base_c + fc * base_s
            c_tile = crow[:, pl.ds(pl.multiple_of(tt * 128, 128), 128)]
            real, imag = [], []
            for g in range(6):
                c = c_tile[8 * g:8 * g + 8, :]
                real.append(raw[pl.ds(g * 8 * RAW + 2 * t, 8, stride=RAW), :] * c)
                imag.append(raw[pl.ds(g * 8 * RAW + 2 * t + 1, 8, stride=RAW), :] * c)
            re_s, im_s, re_b, im_b = [], [], [], []
            for s in range(SHIFTS):
                cs = jnp.broadcast_to(cosine[s:s + 1, :], (8, 128))
                sn = jnp.broadcast_to(sine[s:s + 1, :], (8, 128))
                for g in range(6):
                    ac, bs = real[g] * cs, imag[g] * sn
                    bc, as_ = imag[g] * cs, real[g] * sn
                    re_s.append(ac + bs)
                    im_s.append(bc - as_)
                    re_b.append(ac - bs)
                    im_b.append(bc + as_)
            for dst, parts in ((shifted, (re_s, im_s)), (back, (re_b, im_b))):
                for k, part in enumerate(parts):
                    cols = pl.ds(pl.multiple_of(tt * 256 + k * 128, 128), 128)
                    dst[:, cols] = jnp.concatenate(part, axis=0).astype(BF16)
        last = v == 2
        tc, ts = jnp.where(last, leap_c, turn_c), jnp.where(last, leap_s, turn_s)
        return base_c * tc - base_s * ts, base_s * tc + base_c * ts

    other = (x * 2 + 1 - yh) * 2
    second_slots = []

    def hand_on(chunk):
        first, count = LIB_CHUNKS[chunk]
        rows = pl.ds(first * 4, count * 4)
        for k in range(2):
            arrival(lib_in.at[other + k, rows], first_slots[chunk][0][k]).wait_recv()
        slots = []
        view = lib_in.at[pl.ds(other, 2), rows]
        for d in (1, 3, 2):
            copy = remote(view, view, device((x + d) % 4, y, z, core))
            copy.start()
            sent.append(copy)
            slots.append(copy)
        second_slots.append(slots)

    phase = lax.fori_loop(0, 3, shift_tiles, phase)
    hand_on(0)
    phase = lax.fori_loop(3, 6, shift_tiles, phase)
    hand_on(1)
    phase = lax.fori_loop(6, 12, shift_tiles, phase)

    powers = jnp.zeros((CLASSES, POSES), F32)
    total = jnp.zeros((ROWS, POSES), F32)
    arrival(lib_in.at[0], 1).wait_recv()
    for chunk, (first, count) in enumerate(LIB_CHUNKS):
        rows = pl.ds(first * 4, count * 4)
        for pick_slots in first_slots[chunk][1:]:
            for slot in pick_slots:
                arrival(lib_in.at[0, rows], slot).wait_recv()
        for copy in second_slots[chunk]:
            copy.wait_recv()

        def widen_lib(k, carry):
            lib_f[pl.ds(pl.multiple_of(k * BLOCK + first * 4, 16), count * 4), :] = lib_in[k, rows, :].astype(F32)
            return carry

        lax.fori_loop(0, 16, widen_lib, 0)

        def gather_tiles(i, carry):
            for u in range(4):
                tt = first + i * 4 + u
                halves = []
                for k in range(2):
                    parts = [
                        lib_f[pl.ds(c * BLOCK + tt * 4 + k * 2 + p, 8, stride=2 * BLOCK), :]
                        for c in range(2) for p in range(2)
                    ]
                    halves.append(jnp.concatenate(parts, axis=0))
                cols = pl.ds(pl.multiple_of(tt * 256, 256), 256)
                lib_b[:, cols] = jnp.concatenate(halves, axis=1).astype(BF16)
                cols = pl.ds(pl.multiple_of(tt * 128, 128), 128)
                power_f[:, cols] = halves[0] * halves[0] + halves[1] * halves[1]
            return carry

        lax.fori_loop(0, count // 4, gather_tiles, 0)
        for q in range(4):
            lo, hi = max(first, 9 * q), min(first + count, 9 * q + 9)
            if lo < hi:
                c = ctf[:, pl.ds(pl.multiple_of((9 * q + base + lo) * 128, 128), (hi - lo) * 128)]
                powers = powers + lax.dot_general(
                    c * c, power_f[:, lo * 128:hi * 128], (((1,), (1,)), ((), ())),
                    precision=lax.Precision.HIGHEST, preferred_element_type=F32,
                )
        cols = slice(first * 256, (first + count) * 256)
        total = total + lax.dot_general(
            shifted[:, cols], lib_b[:, cols], (((1,), (1,)), ((), ())), preferred_element_type=F32
        )
    class_power = jnp.zeros((PAIR, POSES), F32)
    for k in range(CLASSES):
        class_power = class_power + jnp.where(klass == float(k), powers[k:k + 1, :], 0.0)
    parts = [total[s * PAIR:(s + 1) * PAIR, :] - 0.5 * class_power for s in range(SHIFTS)]
    for s in range(SHIFTS):
        mine[s * PAIR:(s + 1) * PAIR, 0:POSES] = parts[s]
    score_copy = remote(mine, theirs, pair)
    score_copy.start()
    sent.append(score_copy)
    for g in range(32):
        acc[pl.ds(g * UNIT + 72, 8), :] = jnp.zeros((8, 128), F32)
    score_copy.wait_recv()
    scores = [prec * (parts[s] + theirs[s * PAIR:(s + 1) * PAIR, 0:POSES]) for s in range(SHIFTS)]
    top = scores[0]
    for s in range(1, SHIFTS):
        top = jnp.maximum(top, scores[s])
    top = jnp.max(top, axis=1, keepdims=True)
    mass = jnp.exp(scores[0] - top)
    for s in range(1, SHIFTS):
        mass = mass + jnp.exp(scores[s] - top)
    log_norm = top + jnp.log(jnp.sum(mass, axis=1, keepdims=True))
    weight = jnp.concatenate([jnp.where(live > 0.5, jnp.exp(v - log_norm), 0.0) for v in scores], axis=0).astype(BF16)
    unit = lax.broadcasted_iota(jnp.int32, (POSES, POSES), 0) == lax.broadcasted_iota(jnp.int32, (POSES, POSES), 1)
    weight_t = lax.dot_general(
        unit.astype(F32).astype(BF16), weight, (((1,), (1,)), ((), ())), preferred_element_type=F32
    ).astype(BF16)

    x_sends = []
    for first, count, low, high in CHUNKS:
        rows = pl.ds(low, high - low)

        def sum_quarter(q, carry):
            cols = pl.ds(pl.multiple_of((q * 9 + first) * 256, 256), count * 256)
            part = jnp.dot(weight_t, back[:, cols], preferred_element_type=F32)
            for c in range(2):
                for p in range(2):
                    r = c * 16 + p * 8
                    for k in range(2 * count):
                        row = q * UNIT + first * 8 + (k // 2) * 8 + c * 4 + (k % 2) * 2 + p
                        acc[pl.ds(row, 8, stride=4 * UNIT), :] = part[r:r + 8, k * 128:(k + 1) * 128]
            for d in range(1, 4):
                for h in range(2):
                    at = pl.multiple_of((((x + d) % 4 * 2 + h) * 4 + q) * UNIT + low, 16)
                    x_out[d - 1, h, q, rows, :] = acc[pl.ds(at, high - low), :].astype(BF16)
            return carry

        lax.fori_loop(0, 4, sum_quarter, 0)
        chunk_sends = []
        for d in (2, 1, 3):
            copy = remote(
                x_out.at[d - 1, :, :, rows], x_in.at[d - 1, :, :, rows], device((x + d) % 4, y, z, core)
            )
            copy.start()
            chunk_sends.append(copy)
        x_sends.append(chunk_sends)
        sent += chunk_sends
    shown = jnp.where(live > 0.5, log_norm, 0.0)
    shown = jnp.where(core == 0, shown[0:CAP, :], shown[CAP:PAIR, :])
    r24 = lax.broadcasted_iota(jnp.int32, (CAP, 128), 0)
    norm_ref[...] = jnp.sum(jnp.where(r24 == lane24, shown, 0.0), axis=0, keepdims=True)

    y_sends = []
    for (first, count, low, high), chunk_sends in zip(CHUNKS, x_sends):
        rows = pl.ds(low, high - low)
        for copy in chunk_sends:
            copy.wait_recv()
        for h in range(2):
            for q in range(4):
                at = pl.multiple_of(((x * 2 + h) * 4 + q) * UNIT + low, 16)
                part = acc[pl.ds(at, high - low), :]
                for d in range(3):
                    part = part + x_in[d, h, q, rows, :].astype(F32)
                y_own[h * 4 + q, rows, :] = part
                y_out[h * 4 + q, rows, :] = part.astype(BF16)
        chunk_sends = []
        for d in (4, 3, 5, 2, 6, 1, 7):
            py = (y + d) % 8
            copy = remote(y_out.at[py, rows], y_in.at[d - 1, rows], device(x, py, z, core))
            copy.start()
            chunk_sends.append(copy)
        y_sends.append(chunk_sends)
        sent += chunk_sends
    for (first, count, low, high), chunk_sends in zip(CHUNKS, y_sends):
        rows = pl.ds(low, high - low)
        for copy in chunk_sends:
            copy.wait_recv()
        part = y_own[y, rows, :]
        for d in range(7):
            part = part + y_in[d, rows, :].astype(F32)
        z_own[rows, :] = part

    zeros4 = jnp.zeros((4, 128), F32)
    for k in range(4):
        for c in range(2):
            for i in range(3):
                first = (2 * k + i) * 8 + c * 4
                z_f[2 * k + c, 4 * i:4 * i + 4, :] = z_own[first:first + 4, :]
            z_f[2 * k + c, 12:16, :] = zeros4
            z_out[2 * k + c] = z_f[2 * k + c].astype(BF16)
    z_first = next(recv_slots)
    for _ in range(7):
        next(recv_slots)
    own_place = z // 4 == core
    z_sends = []
    for d in (2, 1, 3, 0):
        k = (z + d) % 4
        for c in (mate, core):
            z_sends.append(remote(
                z_out.at[2 * k + c], z_in.at[z], device(x, y, 4 * core + k, c), z_first + z
            ))
    for copy in z_sends[:-1]:
        copy.start()
    sent += z_sends[:-1]

    @pl.when(own_place)
    def _():
        z_in[z] = z_out[2 * (z % 4) + core]

    @pl.when(jnp.logical_not(own_place))
    def _():
        z_sends[-1].start()

    for k in range(8):
        @pl.when(jnp.logical_not(jnp.logical_and(own_place, z == k)))
        def _():
            arrival(z_in.at[k], z_first + k).wait_recv()

    part = z_in[0].astype(F32)
    for k in range(1, 8):
        part = part + z_in[k].astype(F32)
    skip = (z % 4) * 32
    turned = pltpu.roll(part, (128 - skip) % 128, 1)
    keep = lax.broadcasted_iota(jnp.int32, (4, 128), 1) < 128 - skip
    for t in range(3):
        piece = turned[4 * t:4 * t + 4, :]
        if t < 2:
            piece = jnp.where(keep, piece, turned[4 * t + 4:4 * t + 8, :])
        width = 128 if t < 2 else 32
        for p in range(2):
            for c in range(2):
                accum_ref[p, c:c + 1, t * 128:t * 128 + width] = piece[c * 2 + p:c * 2 + p + 1, 0:width]

    for copy in sent:
        copy.wait_send()

    @pl.when(jnp.logical_not(own_place))
    def _():
        z_sends[-1].wait_send()


def body(images, classes, precision, counts, shifts, ctf_table, projections):
    raw_img = images.reshape(CAP, 2, TILES, 128).transpose(0, 2, 1, 3).reshape(CAP * RAW, 128)
    raw_proj = projections.reshape(2, 2, TILES, 128).transpose(0, 2, 1, 3).reshape(2 * RAW, 128)
    vmem = pl.BlockSpec(memory_space=pltpu.VMEM)
    anywhere = pl.BlockSpec(memory_space=pl.ANY)
    accum, norm = pl.pallas_call(
        kernel,
        out_shape=(
            jax.ShapeDtypeStruct((2, 2, HALF // 32), F32),
            jax.ShapeDtypeStruct((1, 128), F32),
        ),
        in_specs=[anywhere] * 7,
        out_specs=(vmem, vmem),
        scratch_shapes=[
            pltpu.VMEM((1, CAP), jnp.int32),
            pltpu.VMEM((1, CAP), F32),
            pltpu.VMEM((1, 1), jnp.int32),
            pltpu.VMEM((2, SHIFTS), jnp.int32),
            pltpu.VMEM((2 * RAW, 128), BF16),
            pltpu.VMEM((2, CAP * RAW, 128), BF16),
            pltpu.VMEM((CLASSES, HALF), F32),
            pltpu.VMEM((PAIR * RAW, 128), F32),
            pltpu.VMEM((PAIR, HALF // 2), F32),
            pltpu.VMEM((ROWS, HALF), BF16),
            pltpu.VMEM((ROWS, HALF), BF16),
            pltpu.VMEM((2, CAP, 128), F32),
            pltpu.VMEM((2 * RAW, 128), F32),
            pltpu.VMEM((2 * BLOCK, 128), F32),
            pltpu.VMEM((2, BLOCK, 128), BF16),
            pltpu.VMEM((16, BLOCK, 128), BF16),
            pltpu.VMEM((16 * BLOCK, 128), F32),
            pltpu.VMEM((POSES, HALF), BF16),
            pltpu.VMEM((POSES, HALF // 2), F32),
            pltpu.VMEM((ROWS, 128), F32),
            pltpu.VMEM((ROWS, 128), F32),
            pltpu.VMEM((32 * UNIT, 128), F32),
            pltpu.VMEM((3, 2, 4, UNIT, 128), BF16),
            pltpu.VMEM((3, 2, 4, UNIT, 128), BF16),
            pltpu.VMEM((8, UNIT, 128), F32),
            pltpu.VMEM((8, UNIT, 128), BF16),
            pltpu.VMEM((7, UNIT, 128), BF16),
            pltpu.VMEM((UNIT, 128), F32),
            pltpu.VMEM((8, 16, 128), F32),
            pltpu.VMEM((8, 16, 128), BF16),
            pltpu.VMEM((8, 16, 128), BF16),
            pltpu.SemaphoreType.DMA((7,)),
            pltpu.SemaphoreType.DMA((80,)),
            pltpu.SemaphoreType.DMA((80,)),
        ],
        compiler_params=pltpu.CompilerParams(
            collective_id=0, has_side_effects=True, vmem_limit_bytes=56 * 1024 * 1024
        ),
        name="expectation",
    )(
        classes.reshape(1, CAP), precision.reshape(1, CAP), counts.reshape(1, 1), shifts.T,
        raw_img, ctf_table, raw_proj,
    )
    return accum, norm.reshape(128)[:CAP]


def solution(mesh):
    placed = (
        P(("lib", "dom"), None, None),
        P(("lib", "dom")),
        P(("lib", "dom")),
        P(("lib", "dom")),
        P(),
        P(),
        P("lib", None, None),
    )
    return jax.shard_map(
        body,
        mesh=mesh,
        in_specs=placed,
        out_specs=(P("lib", None, "dom"), P(("lib", "dom"))),
        check_vma=False,
    )
```

time: 502 us -> 59 us (0.12)
  the two profiles are of different devices: /device:TPU:4 before, /device:TPU:1 now
where the time goes in v2:
time: 59 us; the launch traced here: 58.8 us
  Pallas kernels  55.1 us (93%)
  local copies, waits for them, and re-layouts  2.46 us (4%)
  between operations  1.29 us (2%)
    pallas_call x1, Pallas kernels, body(): pl.pallas_call(kernel, out_shape=(jax.ShapeDtypeStruct((2, 2, HALF // 32)...  55.1 us
    unnamed x3, local copies, waits for them, and re-layouts  1.95 us

profile of v2, /device:TPU:1, one launch (start us, length us, event | category | flops | bytes accessed | tf_op | source)
XLA Modules:
  0.0 58.8 jit_solution(18185853295145684557)
XLA Ops:
  1.3 55.1 %expectation.1 = (f32[2,2,288]{2,1,0:T(2,128)}, f32[1,128]{1,0:T(1,128)}) custom-call(s32[1,24]{1,0:T(1,128)} %bitcast.20, f32[1,24]{1,0:T(1,128)} %bitcast.21, s32[1,1]{1,0:T(1,128)} %bitcast.16.counts_hbm, s32[2,9]{1,0:T(2,128)} %bitcast.19, bf16[3456,128]{1,0:T(8,128)(2,1)} %bitcast.17, f32[8,9216]{1,0:T(8,128)} %ctf_hbm.1, bf16[288,128]{1,0:T(8,128)(2,1)} %bitcast.18), custom_call_target="tpu_custom_call" | custom-call | tf_op jit(solution)/shard_map/expectation/pallas_call | solution.py:443
  56.3 0.0 copy-start
  56.3 0.7 %copy-done = f32[1,128]{1,0:T(1,128)S(1)} copy-done((f32[1,128]{1,0:T(1,128)S(1)}, f32[1,128]{1,0:T(1,128)}, u32[]{:S(2)}) %copy-start) | copy-done | bytes 536
  57.0 0.5 slice_bitcast_fusion
  57.5 1.3 %copy.13 = f32[2,2,288]{2,1,0:T(2,128)} copy(f32[2,2,288]{2,1,0:T(2,128)} %get-tuple-element.8) | data formatting | bytes 9216
Async XLA Ops:
  56.3 0.7 %copy-start = (f32[1,128]{1,0:T(1,128)S(1)}, f32[1,128]{1,0:T(1,128)}, u32[]{:S(2)}) copy-start(f32[1,128]{1,0:T(1,128)} %get-tuple-element.5) | copy-start | bytes 1540

commit v3 on v2

v3 whole, which is shorter than its diff:
```python
import functools
import math

import jax
import jax.numpy as jnp
import numpy as np
from jax import lax
from jax.experimental import pallas as pl
from jax.experimental.pallas import tpu as pltpu
from jax.sharding import PartitionSpec as P

FREQ = 96
SHIFTS = 9
HALF = 9216
CLASSES = 8
CAP = 24
POSES = 32
TILES = 72
RAW = 2 * TILES
WIDE = 2 * HALF
ROWS = SHIFTS * CAP + 8
HALF_TILES = TILES // 2
BLOCK = HALF_TILES * 4
LIB_CHUNKS = ((0, 12), (12, 12), (24, 12))
STEP = 2.0 * np.pi / (2.0 * FREQ)
CHUNKS = ((0, 2), (2, 2), (4, 2), (6, 2), (8, 1))
MESH = pl.DeviceIdType.MESH
F32 = jnp.float32
BF16 = jnp.bfloat16


def place():
    lib = lax.axis_index("lib")
    dom = lax.axis_index("dom")
    return lib // 4, (lib // 2) % 2, dom // 8, dom % 8, lib % 2


def device(x, y, z, core):
    return ((x * 2 + y // 4) * 2 + core, (y % 4) * 8 + z)


def kernel(
    classes_hbm, precision_hbm, counts_hbm, shifts_hbm, img_hbm, ctf_hbm, proj_hbm,
    accum_ref, norm_ref,
    classes_v, precision_v, counts_v, shifts_v, proj,
    img, ctf, raw, crow, phases, shifted, back, meta, own_f, own_r, own_b, lib_in, lib_f, lib_b, power_f,
    mine, theirs, acc, x_out, x_in, y_own, y_out, y_in, z_own, z_f, z_out, z_in,
    local_sem, send_sem, recv_sem,
):
    x, yh, yl, z, core = place()
    y = yh * 4 + yl
    me = (x * 2 + yh) * 2 + core
    mate = 1 - core
    pair = device(x, y, z, mate)
    edge = jnp.logical_or(yl == 0, yl == 3)
    near = jnp.where(yl < 2, y + 7 - yl, y + 4 - yl) % 8
    beyond = [jnp.where(yl == 0, y + 7 - k, y + 1 + k) % 8 for k in range(2)]
    base = core * 9
    send_slots, recv_slots = iter(range(200)), iter(range(200))

    def remote(src, dst, target, recv=None):
        recv = next(recv_slots) if recv is None else recv
        return pltpu.make_async_remote_copy(
            src_ref=src, dst_ref=dst, send_sem=send_sem.at[next(send_slots)], recv_sem=recv_sem.at[recv],
            device_id=target, device_id_type=MESH,
        )

    def arrival(dst, recv):
        return pltpu.make_async_remote_copy(
            src_ref=dst, dst_ref=dst, send_sem=send_sem.at[0], recv_sem=recv_sem.at[recv],
            device_id=pair, device_id_type=MESH,
        )

    sources = [device((x + d) % 4, y, z, c) for d in (1, 2, 3) for c in (0, 1)]
    sources += [device(x, near, z, mate)]
    sources += [device(x, (y + d) % 8, z, core) for d in range(1, 8)]
    sources += [device(x, y, (z + d) % 8, z // 4) for d in range(1, 8)]
    barrier = pltpu.get_barrier_semaphore()
    pl.semaphore_signal(barrier, inc=1, device_id=pair, device_id_type=MESH)
    for source in sources:
        pl.semaphore_signal(barrier, inc=1, device_id=source, device_id_type=MESH)
    copies = [
        pltpu.make_async_copy(src, dst, local_sem.at[k])
        for k, (src, dst) in enumerate((
            (proj_hbm, proj), (classes_hbm, classes_v), (precision_hbm, precision_v), (counts_hbm, counts_v),
            (shifts_hbm, shifts_v), (ctf_hbm, ctf), (img_hbm, img.at[core]),
        ))
    ]
    for copy in copies:
        copy.start()

    def column_of(row, size):
        r = lax.broadcasted_iota(jnp.int32, (size, row.shape[1]), 0)
        c = lax.broadcasted_iota(jnp.int32, (size, row.shape[1]), 1)
        return jnp.sum(jnp.where(r == c, jnp.broadcast_to(row, r.shape), 0.0), axis=1, keepdims=True)

    copies[0].wait()
    own_f[...] = proj[...].astype(F32)
    for h in range(2):
        for q in range(4):
            for p in range(2):
                for c in range(2):
                    rows = own_f[pl.ds(p * RAW + 36 * q + 18 * h + c, 9, stride=2), :]
                    own_r[pl.ds(h * BLOCK + 36 * q + 2 * c + p, 9, stride=4), :] = rows
    own_b[0] = own_r[0:BLOCK, :].astype(BF16)
    own_b[1] = own_r[BLOCK:2 * BLOCK, :].astype(BF16)
    lib_in[me] = own_b[core]

    pl.semaphore_wait(barrier, 14 + jnp.where(z // 4 == core, 6, 8) + jnp.where(edge, 2, 0))

    sent = []
    meta_copy = remote(meta.at[core], meta.at[core], pair)
    block_copy = remote(own_b.at[mate], lib_in.at[me], pair)
    img_copy = remote(img_hbm, img.at[core], pair)
    far_sends, far_slots, first_slots, second_slots = [], [], [], []
    for first, count in LIB_CHUNKS:
        rows = pl.ds(first * 4, count * 4)
        pick = [next(recv_slots), next(recv_slots)]
        far_slots.append(pick)
        for py in (beyond[1], beyond[0]):
            for h in range(2):
                far_sends.append(
                    remote(own_b.at[h, rows], lib_in.at[me, rows], device(x, py, z, h), pick[0] + core)
                )

    @pl.when(edge)
    def _():
        for copy in far_sends:
            copy.start()

    for first, count in LIB_CHUNKS:
        rows = pl.ds(first * 4, count * 4)
        for d in (2, 1, 3):
            pick = [next(recv_slots), next(recv_slots)]
            first_slots.append(pick)
            for h in range(2):
                copy = remote(
                    own_b.at[h, rows], lib_in.at[me, rows], device((x + d) % 4, y, z, h), pick[0] + core
                )
                copy.start()
                sent.append(copy)
    for copy in (block_copy, img_copy):
        copy.start()
        sent.append(copy)

    for copy in copies[1:4]:
        copy.wait()

    lane24 = lax.broadcasted_iota(jnp.int32, (CAP, 128), 1)
    alive = lax.broadcasted_iota(jnp.int32, (CAP, 1), 0) < counts_v[...]
    meta[core] = jnp.where(
        lane24 == 0, column_of(classes_v[...].astype(F32), CAP),
        jnp.where(lane24 == 1, column_of(precision_v[...], CAP), jnp.where(alive, 1.0, 0.0)),
    )
    def prepare(who):
        klass = meta[who][:, 0:1]
        kinds = lax.broadcasted_iota(jnp.int32, (CAP, CLASSES), 1).astype(F32)
        onehot = (klass == kinds).astype(F32)
        pick = jnp.concatenate([onehot, onehot, onehot], axis=1).astype(BF16)
        for q in range(4):
            c = ctf[:, pl.ds(pl.multiple_of((18 * q + base) * 128, 128), 1152)]
            hi = c.astype(BF16).astype(F32)
            mid = (c - hi).astype(BF16).astype(F32)
            low = c - hi - mid
            parts = jnp.concatenate([hi, mid, low], axis=0).astype(BF16)
            crow[:, q * 1152:(q + 1) * 1152] = jnp.dot(pick, parts, preferred_element_type=F32)

        def widen(n, carry):
            rows = pl.ds(pl.multiple_of(n * RAW, 16), RAW)
            raw[rows, :] = img[who, rows, :].astype(F32)
            return carry

        lax.fori_loop(0, CAP, widen, 0)

    zeros8 = jnp.zeros((8, 128), F32)

    def shift_tiles(who, i, carry):
        q, v = i // 3, i % 3
        for u in range(3):
            t = 18 * q + base + 3 * v + u
            tt = 3 * i + u
            cols = pl.ds(pl.multiple_of(tt * 128, 128), 128)
            real, imag = [], []
            for g in range(3):
                c = crow[8 * g:8 * g + 8, cols]
                real.append(raw[pl.ds(g * 8 * RAW + 2 * t, 8, stride=RAW), :] * c)
                imag.append(raw[pl.ds(g * 8 * RAW + 2 * t + 1, 8, stride=RAW), :] * c)
            pairs = []
            for k in range(SHIFTS * 3 + 1):
                s, g = k // 3, k % 3
                if s < SHIFTS:
                    if g == 0:
                        cs = jnp.broadcast_to(phases[0, pl.ds(s, 1), cols], (8, 128))
                        sn = jnp.broadcast_to(phases[1, pl.ds(s, 1), cols], (8, 128))
                    ac, bs = real[g] * cs, imag[g] * sn
                    bc, as_ = imag[g] * cs, real[g] * sn
                    pairs.append((ac + bs, bc - as_, ac - bs, bc + as_))
                else:
                    pairs.append((zeros8,) * 4)
                if k % 2:
                    for j, (dst, half) in enumerate(((shifted, 0), (shifted, 1), (back, 0), (back, 1))):
                        wide = pl.ds(pl.multiple_of(tt * 256 + half * 128, 128), 128)
                        both = jnp.concatenate([pairs[0][j], pairs[1][j]], axis=0).astype(BF16)
                        dst[who, pl.ds(8 * (k - 1), 16), wide] = both
                    pairs = []
        return carry

    meta_copy.start()
    sent.append(meta_copy)


    copies[4].wait()
    step = shifts_v[...].astype(F32)
    step_x = jnp.broadcast_to(column_of(step[0:1, :], 16), (16, 128))
    step_y = jnp.broadcast_to(column_of(step[1:2, :], 16), (16, 128))
    fine = []
    lanes = lax.broadcasted_iota(jnp.int32, (16, 128), 1)

    def turned_by(steps):
        steps = steps - 192.0 * jnp.floor(steps * (1.0 / 192.0) + 0.5)
        h = steps * (0.5 * STEP)
        h2 = h * h
        sn, cs = jnp.zeros_like(h), jnp.zeros_like(h)
        for k in range(7, -1, -1):
            sn = sn * h2 + (-1.0) ** k / math.factorial(2 * k + 1)
            cs = cs * h2 + (-1.0) ** k / math.factorial(2 * k)
        sn = sn * h
        return 1.0 - 2.0 * (sn * sn), 2.0 * (sn * cs)

    for u in range(3):
        j = lanes + u * 128
        dy = (j >= 96).astype(jnp.int32) + (j >= 192).astype(jnp.int32) + (j >= 288).astype(jnp.int32)
        kx = j - 96 * dy
        fine.append(turned_by(step_x * kx.astype(F32) + step_y * dy.astype(F32)))
    rows_on = jnp.where(lanes == 0, 12 * core - FREQ // 2, jnp.where(lanes == 1, 4, 16)).astype(F32)
    coarse = turned_by(step_y * rows_on)
    start_c, turn_c, leap_c = [jnp.broadcast_to(coarse[0][:, k:k + 1], (16, 128)) for k in range(3)]
    start_s, turn_s, leap_s = [jnp.broadcast_to(coarse[1][:, k:k + 1], (16, 128)) for k in range(3)]

    def table(i, carry):
        base_c, base_s = carry
        for u in range(3):
            fc, fs = fine[u]
            cols = pl.ds(pl.multiple_of((3 * i + u) * 128, 128), 128)
            phases[0, :, cols] = fc * base_c - fs * base_s
            phases[1, :, cols] = fs * base_c + fc * base_s
        last = i % 3 == 2
        tc, ts = jnp.where(last, leap_c, turn_c), jnp.where(last, leap_s, turn_s)
        return base_c * tc - base_s * ts, base_s * tc + base_c * ts

    lax.fori_loop(0, 12, table, (start_c, start_s))

    copies[5].wait()
    copies[6].wait()
    prepare(core)

    other = (x * 2 + 1 - yh) * 2

    def hand_on(chunk):
        first, count = LIB_CHUNKS[chunk]
        rows = pl.ds(first * 4, count * 4)
        for k in range(2):
            arrival(lib_in.at[other + k, rows], far_slots[chunk][k]).wait_recv()
        slots = []
        view = lib_in.at[pl.ds(other, 2), rows]
        for d in (2, 1, 3):
            copy = remote(view, view, device((x + d) % 4, y, z, core))
            copy.start()
            sent.append(copy)
            slots.append(copy)
        second_slots.append(slots)

    lax.fori_loop(0, 12, functools.partial(shift_tiles, core), 0, unroll=2)

    hand_on(0)

    arrival(meta.at[mate], 0).wait_recv()
    arrival(img.at[mate], 2).wait_recv()
    prepare(mate)
    lax.fori_loop(0, 2, functools.partial(shift_tiles, mate), 0, unroll=2)
    hand_on(1)
    lax.fori_loop(2, 6, functools.partial(shift_tiles, mate), 0, unroll=2)
    hand_on(2)
    lax.fori_loop(6, 12, functools.partial(shift_tiles, mate), 0, unroll=2)

    powers = jnp.zeros((CLASSES, POSES), F32)
    total = [jnp.zeros((ROWS, POSES), F32)] * 2
    arrival(lib_in.at[0], 1).wait_recv()
    for chunk, (first, count) in enumerate(LIB_CHUNKS):
        rows = pl.ds(first * 4, count * 4)
        for pick in first_slots[3 * chunk:3 * chunk + 3]:
            for slot in pick:
                arrival(lib_in.at[0, rows], slot).wait_recv()
        for copy in second_slots[chunk]:
            copy.wait_recv()

        def widen_lib(k, carry):
            lib_f[pl.ds(pl.multiple_of(k * BLOCK + first * 4, 16), count * 4), :] = lib_in[k, rows, :].astype(F32)
            return carry

        lax.fori_loop(0, 16, widen_lib, 0)

        def gather_tiles(i, carry):
            for u in range(4):
                tt = first + i * 4 + u
                halves = []
                for k in range(2):
                    parts = [
                        lib_f[pl.ds(c * BLOCK + tt * 4 + k * 2 + p, 8, stride=2 * BLOCK), :]
                        for c in range(2) for p in range(2)
                    ]
                    halves.append(jnp.concatenate(parts, axis=0))
                cols = pl.ds(pl.multiple_of(tt * 256, 256), 256)
                lib_b[:, cols] = jnp.concatenate(halves, axis=1).astype(BF16)
                cols = pl.ds(pl.multiple_of(tt * 128, 128), 128)
                power_f[:, cols] = halves[0] * halves[0] + halves[1] * halves[1]
            return carry

        lax.fori_loop(0, count // 4, gather_tiles, 0)
        for q in range(4):
            lo, hi = max(first, 9 * q), min(first + count, 9 * q + 9)
            if lo < hi:
                c = ctf[:, pl.ds(pl.multiple_of((9 * q + base + lo) * 128, 128), (hi - lo) * 128)]
                powers = powers + lax.dot_general(
                    c * c, power_f[:, lo * 128:hi * 128], (((1,), (1,)), ((), ())),
                    precision=lax.Precision.HIGHEST, preferred_element_type=F32,
                )
        cols = slice(first * 256, (first + count) * 256)
        for c in range(2):
            total[c] = total[c] + lax.dot_general(
                shifted[c, :, cols], lib_b[:, cols], (((1,), (1,)), ((), ())), preferred_element_type=F32
            )
    klass = [meta[c][:, 0:1] for c in range(2)]
    parts = []
    for c in range(2):
        class_power = jnp.zeros((CAP, POSES), F32)
        for k in range(CLASSES):
            class_power = class_power + jnp.where(klass[c] == float(k), powers[k:k + 1, :], 0.0)
        parts.append([total[c][s * CAP:(s + 1) * CAP, :] - 0.5 * class_power for s in range(SHIFTS)])
        for s in range(SHIFTS):
            mine[c, s * CAP:(s + 1) * CAP, 0:POSES] = parts[c][s]
    score_copy = remote(mine, theirs, pair)
    score_copy.start()
    sent.append(score_copy)
    score_copy.wait_recv()
    log_norm, weights = [], []
    for c in range(2):
        prec, live = meta[c][:, 1:2], meta[c][:, 2:3] > 0.5
        scores = [prec * (parts[c][s] + theirs[c, s * CAP:(s + 1) * CAP, 0:POSES]) for s in range(SHIFTS)]
        top = scores[0]
        for s in range(1, SHIFTS):
            top = jnp.maximum(top, scores[s])
        top = jnp.max(top, axis=1, keepdims=True)
        mass = jnp.exp(scores[0] - top)
        for s in range(1, SHIFTS):
            mass = mass + jnp.exp(scores[s] - top)
        norm = top + jnp.log(jnp.sum(mass, axis=1, keepdims=True))
        log_norm.append(jnp.where(live, norm, 0.0))
        weights += [jnp.where(live, jnp.exp(v - norm), 0.0) for v in scores] + [jnp.zeros((8, POSES), F32)]
    weight = jnp.concatenate(weights, axis=0).astype(BF16)
    unit = lax.broadcasted_iota(jnp.int32, (POSES, POSES), 0) == lax.broadcasted_iota(jnp.int32, (POSES, POSES), 1)
    weight_t = lax.dot_general(
        unit.astype(F32).astype(BF16), weight, (((1,), (1,)), ((), ())), preferred_element_type=F32
    ).astype(BF16)

    x_sends = []
    for first, count in CHUNKS:
        rows = pl.ds(64 * first, 64 * count)

        def sum_quarter(q, carry):
            cols = pl.ds(pl.multiple_of((q * 9 + first) * 256, 256), count * 256)
            part = jnp.dot(weight_t[:, 0:ROWS], back[0, :, cols], preferred_element_type=F32)
            part = part + jnp.dot(weight_t[:, ROWS:2 * ROWS], back[1, :, cols], preferred_element_type=F32)
            for c in range(2):
                for p in range(2):
                    r = c * 16 + p * 8
                    for k in range(2 * count):
                        row = 256 * first + (q * count + k // 2) * 8 + c * 4 + (k % 2) * 2 + p
                        acc[pl.ds(row, 8, stride=32 * count), :] = part[r:r + 8, k * 128:(k + 1) * 128]
            return carry

        lax.fori_loop(0, 4, sum_quarter, 0)
        chunk_sends = []
        for d in (2, 1, 3):
            at = pl.multiple_of(256 * first + (x + d) % 4 * 64 * count, 64)
            x_out[d - 1, rows, :] = acc[pl.ds(at, 64 * count), :].astype(BF16)
            copy = remote(x_out.at[d - 1, rows], x_in.at[d - 1, rows], device((x + d) % 4, y, z, core))
            copy.start()
            chunk_sends.append(copy)
        x_sends.append(chunk_sends)
        sent += chunk_sends
    shown = jnp.where(core == 0, log_norm[0], log_norm[1])
    r24 = lax.broadcasted_iota(jnp.int32, (CAP, 128), 0)
    norm_ref[...] = jnp.sum(jnp.where(r24 == lane24, shown, 0.0), axis=0, keepdims=True)

    y_sends = []
    for (first, count), chunk_sends in zip(CHUNKS, x_sends):
        rows = pl.ds(64 * first, 64 * count)
        size = 8 * count
        for copy in chunk_sends:
            copy.wait_recv()
        part = acc[pl.ds(pl.multiple_of(256 * first + x * 64 * count, 64), 64 * count), :]
        for d in range(3):
            part = part + x_in[d, rows, :].astype(F32)
        room = pl.ds(8 * first, max(size, 16))
        for g in range(8):
            piece = part[g * size:(g + 1) * size, :]
            y_own[g, pl.ds(8 * first, size), :] = piece
            if size < 16:
                piece = jnp.concatenate([piece, zeros8], axis=0)
            y_out[g, room, :] = piece.astype(BF16)
        chunk_sends = []
        for d in (4, 3, 5, 2, 6, 1, 7):
            py = (y + d) % 8
            copy = remote(y_out.at[py, room], y_in.at[d - 1, room], device(x, py, z, core))
            copy.start()
            chunk_sends.append(copy)
        y_sends.append(chunk_sends)
        sent += chunk_sends
    for (first, count), chunk_sends in zip(CHUNKS, y_sends):
        size = 8 * count
        for copy in chunk_sends:
            copy.wait_recv()
        part = y_own[y, pl.ds(8 * first, size), :]
        for d in range(7):
            part = part + y_in[d, pl.ds(8 * first, max(size, 16)), :].astype(F32)[0:size, :]
        z_own[pl.ds(8 * first, size), :] = part

    zeros4 = jnp.zeros((4, 128), F32)
    for k in range(4):
        for c in range(2):
            for i in range(3):
                first = (2 * k + i) * 8 + c * 4
                z_f[2 * k + c, 4 * i:4 * i + 4, :] = z_own[first:first + 4, :]
            z_f[2 * k + c, 12:16, :] = zeros4
            z_out[2 * k + c] = z_f[2 * k + c].astype(BF16)
    z_first = next(recv_slots)
    for _ in range(7):
        next(recv_slots)
    own_place = z // 4 == core
    z_sends = []
    for d in (2, 1, 3, 0):
        k = (z + d) % 4
        for c in (mate, core):
            z_sends.append(remote(
                z_out.at[2 * k + c], z_in.at[z], device(x, y, 4 * core + k, c), z_first + z
            ))
    for copy in z_sends[:-1]:
        copy.start()
    sent += z_sends[:-1]

    @pl.when(own_place)
    def _():
        z_in[z] = z_out[2 * (z % 4) + core]

    @pl.when(jnp.logical_not(own_place))
    def _():
        z_sends[-1].start()

    for k in range(8):
        @pl.when(jnp.logical_not(jnp.logical_and(own_place, z == k)))
        def _():
            arrival(z_in.at[k], z_first + k).wait_recv()

    part = z_in[0].astype(F32)
    for k in range(1, 8):
        part = part + z_in[k].astype(F32)
    skip = (z % 4) * 32
    turned = pltpu.roll(part, (128 - skip) % 128, 1)
    keep = lax.broadcasted_iota(jnp.int32, (4, 128), 1) < 128 - skip
    for t in range(3):
        piece = turned[4 * t:4 * t + 4, :]
        if t < 2:
            piece = jnp.where(keep, piece, turned[4 * t + 4:4 * t + 8, :])
        for p in range(2):
            for c in range(2):
                accum_ref[p, c:c + 1, t * 128:t * 128 + 128] = piece[c * 2 + p:c * 2 + p + 1, :]

    for copy in sent:
        copy.wait_send()

    @pl.when(edge)
    def _():
        for copy in far_sends:
            copy.wait_send()

    @pl.when(jnp.logical_not(own_place))
    def _():
        z_sends[-1].wait_send()


def body(images, classes, precision, counts, shifts, ctf_table, projections):
    raw_img = images.reshape(CAP, 2, TILES, 128).transpose(0, 2, 1, 3).reshape(CAP * RAW, 128)
    raw_proj = projections.reshape(2, 2, TILES, 128).transpose(0, 2, 1, 3).reshape(2 * RAW, 128)
    vmem = pl.BlockSpec(memory_space=pltpu.VMEM)
    anywhere = pl.BlockSpec(memory_space=pl.ANY)
    accum, norm = pl.pallas_call(
        kernel,
        out_shape=(
            jax.ShapeDtypeStruct((2, 2, 384), F32),
            jax.ShapeDtypeStruct((1, 128), F32),
        ),
        in_specs=[anywhere] * 7,
        out_specs=(vmem, vmem),
        scratch_shapes=[
            pltpu.VMEM((1, CAP), jnp.int32),
            pltpu.VMEM((1, CAP), F32),
            pltpu.VMEM((1, 1), jnp.int32),
            pltpu.VMEM((2, SHIFTS), jnp.int32),
            pltpu.VMEM((2 * RAW, 128), BF16),
            pltpu.VMEM((2, CAP * RAW, 128), BF16),
            pltpu.VMEM((CLASSES, HALF), F32),
            pltpu.VMEM((CAP * RAW, 128), F32),
            pltpu.VMEM((CAP, HALF // 2), F32),
            pltpu.VMEM((2, 16, HALF // 2), F32),
            pltpu.VMEM((2, ROWS, HALF), BF16),
            pltpu.VMEM((2, ROWS, HALF), BF16),
            pltpu.VMEM((2, CAP, 128), F32),
            pltpu.VMEM((2 * RAW, 128), F32),
            pltpu.VMEM((2 * BLOCK, 128), F32),
            pltpu.VMEM((2, BLOCK, 128), BF16),
            pltpu.VMEM((16, BLOCK, 128), BF16),
            pltpu.VMEM((16 * BLOCK, 128), F32),
            pltpu.VMEM((POSES, HALF), BF16),
            pltpu.VMEM((POSES, HALF // 2), F32),
            pltpu.VMEM((2, ROWS, 128), F32),
            pltpu.VMEM((2, ROWS, 128), F32),
            pltpu.VMEM((32 * 72, 128), F32),
            pltpu.VMEM((3, 576, 128), BF16),
            pltpu.VMEM((3, 576, 128), BF16),
            pltpu.VMEM((8, 72, 128), F32),
            pltpu.VMEM((8, 80, 128), BF16),
            pltpu.VMEM((7, 80, 128), BF16),
            pltpu.VMEM((72, 128), F32),
            pltpu.VMEM((8, 16, 128), F32),
            pltpu.VMEM((8, 16, 128), BF16),
            pltpu.VMEM((8, 16, 128), BF16),
            pltpu.SemaphoreType.DMA((7,)),
            pltpu.SemaphoreType.DMA((128,)),
            pltpu.SemaphoreType.DMA((128,)),
        ],
        compiler_params=pltpu.CompilerParams(
            collective_id=0, has_side_effects=True, vmem_limit_bytes=56 * 1024 * 1024
        ),
        name="expectation",
    )(
        classes.reshape(1, CAP), precision.reshape(1, CAP), counts.reshape(1, 1), shifts.T,
        raw_img, ctf_table, raw_proj,
    )
    return accum[:, :, :HALF // 32], norm.reshape(128)[:CAP]


def solution(mesh):
    placed = (
        P(("lib", "dom"), None, None),
        P(("lib", "dom")),
        P(("lib", "dom")),
        P(("lib", "dom")),
        P(),
        P(),
        P("lib", None, None),
    )
    return jax.shard_map(
        body,
        mesh=mesh,
        in_specs=placed,
        out_specs=(P("lib", None, "dom"), P(("lib", "dom"))),
        check_vma=False,
    )
```

time: 59 us -> 54.5 us (0.924)
  Pallas kernels: 55.1 us -> 51.2 us
  local copies, waits for them, and re-layouts: 2.46 us -> 1.78 us
    pallas_call x1, Pallas kernels: 55.1 us -> 51.2 us  [body(): pl.pallas_call(kernel, out_shape=(jax.ShapeDtypeStruct((2, 2, 384), F32),...]
    unnamed x3, local copies, waits for them, and re-layouts: 1.95 us -> 0.6 us
    slice x1, local copies, waits for them, and re-layouts: 0.51 us -> 1.18 us  [body(): return (accum[:, :, :HALF // 32], norm.reshape(128)[:CAP])]
where the time goes in v3:
time: 54.5 us; the launch traced here: 54.3 us
  Pallas kernels  51.2 us (94%)
  local copies, waits for them, and re-layouts  1.78 us (3%)
  between operations  1.29 us (2%)
    pallas_call x1, Pallas kernels, body(): pl.pallas_call(kernel, out_shape=(jax.ShapeDtypeStruct((2, 2, 384), F32),...  51.2 us
    slice x1, local copies, waits for them, and re-layouts, body(): return (accum[:, :, :HALF // 32], norm.reshape(128)[:CAP])  1.18 us

profile of v3, /device:TPU:1, one launch (start us, length us, event | category | flops | bytes accessed | tf_op | source)
XLA Modules:
  0.0 54.3 jit_solution(14065965661650182578)
XLA Ops:
  1.3 51.2 %expectation.1 = (f32[2,2,384]{2,1,0:T(2,128)}, f32[1,128]{1,0:T(1,128)}) custom-call(s32[1,24]{1,0:T(1,128)} %bitcast.22, f32[1,24]{1,0:T(1,128)} %bitcast.23, s32[1,1]{1,0:T(1,128)} %bitcast.17.counts_hbm, s32[2,9]{1,0:T(2,128)} %bitcast.21, bf16[3456,128]{1,0:T(8,128)(2,1)} %bitcast.18, f32[8,9216]{1,0:T(8,128)} %ctf_hbm.1, bf16[288,128]{1,0:T(8,128)(2,1)} %bitcast.19), custom_call_target="tpu_custom_call" | custom-call | tf_op jit(solution)/shard_map/expectation/pallas_call | solution.py:497
  52.5 0.0 copy-start
  52.5 1.2 %slice_bitcast_fusion = f32[24]{0:T(128)} fusion(f32[1,128]{1,0:T(1,128)} %get-tuple-element.5), kind=kLoop, calls=%fused_computation | loop fusion | bytes 192 | tf_op jit(solution)/shard_map/slice | solution.py:550
  53.7 0.0 copy-done
  53.7 0.6 %copy.13 = f32[2,2,288]{2,1,0:T(2,128)} copy(f32[2,2,288]{2,1,0:T(2,128)S(1)} %bitcast.20) | data formatting | bytes 9216
Async XLA Ops:
  52.5 1.2 %copy-start = (f32[2,2,384]{2,1,0:T(2,128)S(1)}, f32[2,2,384]{2,1,0:T(2,128)}, u32[]{:S(2)}) copy-start(f32[2,2,384]{2,1,0:T(2,128)} %get-tuple-element.4) | copy-start | bytes 18436

commit v4 on v3

--- a/solution.py
+++ b/solution.py
@@ -21,9 +21,11 @@
 ROWS = SHIFTS * CAP + 8
 HALF_TILES = TILES // 2
 BLOCK = HALF_TILES * 4
-LIB_CHUNKS = ((0, 12), (12, 12), (24, 12))
+LIB_CHUNKS = ((0, 12, 48), (12, 12, 48), (24, 12, 64))
+FULL = BLOCK + 16
 STEP = 2.0 * np.pi / (2.0 * FREQ)
-CHUNKS = ((0, 2), (2, 2), (4, 2), (6, 2), (8, 1))
+CHUNKS = ((2, 2), (4, 2), (6, 2), (8, 1))
+LEAD = 2
 MESH = pl.DeviceIdType.MESH
 F32 = jnp.float32
 BF16 = jnp.bfloat16
@@ -43,8 +45,8 @@
     classes_hbm, precision_hbm, counts_hbm, shifts_hbm, img_hbm, ctf_hbm, proj_hbm,
     accum_ref, norm_ref,
     classes_v, precision_v, counts_v, shifts_v, proj,
-    img, ctf, raw, crow, phases, shifted, back, meta, own_f, own_r, own_b, lib_in, lib_f, lib_b, power_f,
-    mine, theirs, acc, x_out, x_in, y_own, y_out, y_in, z_own, z_f, z_out, z_in,
+    img, ctf, raw, crow, phases, shifted, back, meta, own_f, own_r, own_p, own_b, lib_in, lib_f, lib_b,
+    mine, theirs, acc, x_out, x_in, y_own, y_out, y_in, lead_out, lead_in, last_own, last_out, last_in, z_own, z_f, z_out, z_in,
     local_sem, send_sem, recv_sem,
 ):
     x, yh, yl, z, core = place()
@@ -71,6 +73,15 @@
             device_id=pair, device_id_type=MESH,
         )
 
+    copies = [
+        pltpu.make_async_copy(src, dst, local_sem.at[k])
+        for k, (src, dst) in enumerate((
+            (proj_hbm, proj), (classes_hbm, classes_v), (precision_hbm, precision_v), (counts_hbm, counts_v),
+            (shifts_hbm, shifts_v), (ctf_hbm, ctf), (img_hbm, img.at[core]),
+        ))
+    ]
+    copies[0].start()
+
     sources = [device((x + d) % 4, y, z, c) for d in (1, 2, 3) for c in (0, 1)]
     sources += [device(x, near, z, mate)]
     sources += [device(x, (y + d) % 8, z, core) for d in range(1, 8)]
@@ -79,14 +90,7 @@
     pl.semaphore_signal(barrier, inc=1, device_id=pair, device_id_type=MESH)
     for source in sources:
         pl.semaphore_signal(barrier, inc=1, device_id=source, device_id_type=MESH)
-    copies = [
-        pltpu.make_async_copy(src, dst, local_sem.at[k])
-        for k, (src, dst) in enumerate((
-            (proj_hbm, proj), (classes_hbm, classes_v), (precision_hbm, precision_v), (counts_hbm, counts_v),
-            (shifts_hbm, shifts_v), (ctf_hbm, ctf), (img_hbm, img.at[core]),
-        ))
-    ]
-    for copy in copies:
+    for copy in copies[1:]:
         copy.start()
 
     def column_of(row, size):
@@ -102,9 +106,8 @@
                 for c in range(2):
                     rows = own_f[pl.ds(p * RAW + 36 * q + 18 * h + c, 9, stride=2), :]
                     own_r[pl.ds(h * BLOCK + 36 * q + 2 * c + p, 9, stride=4), :] = rows
-    own_b[0] = own_r[0:BLOCK, :].astype(BF16)
-    own_b[1] = own_r[BLOCK:2 * BLOCK, :].astype(BF16)
-    lib_in[me] = own_b[core]
+    for h in range(2):
+        own_b[h, 0:BLOCK, :] = own_r[h * BLOCK:(h + 1) * BLOCK, :].astype(BF16)
 
     pl.semaphore_wait(barrier, 14 + jnp.where(z // 4 == core, 6, 8) + jnp.where(edge, 2, 0))
 
@@ -113,8 +116,8 @@
     block_copy = remote(own_b.at[mate], lib_in.at[me], pair)
     img_copy = remote(img_hbm, img.at[core], pair)
     far_sends, far_slots, first_slots, second_slots = [], [], [], []
-    for first, count in LIB_CHUNKS:
-        rows = pl.ds(first * 4, count * 4)
+    for first, count, length in LIB_CHUNKS:
+        rows = pl.ds(first * 4, length)
         pick = [next(recv_slots), next(recv_slots)]
         far_slots.append(pick)
         for py in (beyond[1], beyond[0]):
@@ -125,11 +128,12 @@
 
     @pl.when(edge)
     def _():
-        for copy in far_sends:
+        for copy in far_sends[:8]:
             copy.start()
 
-    for first, count in LIB_CHUNKS:
-        rows = pl.ds(first * 4, count * 4)
+    def to_peers(chunk):
+        first, count, length = LIB_CHUNKS[chunk]
+        rows = pl.ds(first * 4, length)
         for d in (2, 1, 3):
             pick = [next(recv_slots), next(recv_slots)]
             first_slots.append(pick)
@@ -139,6 +143,42 @@
                 )
                 copy.start()
                 sent.append(copy)
+
+    to_peers(0)
+    to_peers(1)
+
+    copies[5].wait()
+    lane8 = lax.broadcasted_iota(jnp.int32, (8, 128), 1)
+    tile = jnp.zeros((8, 128), F32)
+    for p in range(2):
+        re = own_f[pl.ds(p * RAW, TILES, stride=2), :]
+        im = own_f[pl.ds(p * RAW + 1, TILES, stride=2), :]
+        own_p[p] = re * re + im * im
+    sums = [jnp.zeros((8, 128), F32)] * 8
+    for t in range(TILES):
+        c = ctf[:, t * 128:(t + 1) * 128]
+        c = c * c
+        for p in range(2):
+            k = 2 * (t % 4) + p
+            sums[k] = sums[k] + c * jnp.broadcast_to(own_p[p, pl.ds(t, 1), :], (8, 128))
+    for p in range(2):
+        power = jnp.sum((sums[p] + sums[2 + p]) + (sums[4 + p] + sums[6 + p]), axis=1, keepdims=True)
+        hi = power.astype(BF16).astype(F32)
+        mid = (power - hi).astype(BF16).astype(F32)
+        column = core * 16 + p * 8 + x * 2 + yh
+        for k, part in enumerate((hi, mid, power - hi - mid)):
+            tile = tile + jnp.where(lane8 == column + 32 * k, part, 0.0)
+    tile = jnp.concatenate([tile, jnp.zeros((8, 128), F32)], axis=0).astype(BF16)
+    own_b[0, pl.ds(BLOCK, 16), :] = tile
+    own_b[1, pl.ds(BLOCK, 16), :] = tile
+
+    @pl.when(edge)
+    def _():
+        for copy in far_sends[8:]:
+            copy.start()
+
+    to_peers(2)
+    lib_in[me] = own_b[core]
     for copy in (block_copy, img_copy):
         copy.start()
         sent.append(copy)
@@ -152,6 +192,11 @@
         lane24 == 0, column_of(classes_v[...].astype(F32), CAP),
         jnp.where(lane24 == 1, column_of(precision_v[...], CAP), jnp.where(alive, 1.0, 0.0)),
     )
+    def three_parts(v):
+        hi = v.astype(BF16).astype(F32)
+        mid = (v - hi).astype(BF16).astype(F32)
+        return jnp.concatenate([hi, mid, v - hi - mid], axis=0).astype(BF16)
+
     def prepare(who):
         klass = meta[who][:, 0:1]
         kinds = lax.broadcasted_iota(jnp.int32, (CAP, CLASSES), 1).astype(F32)
@@ -159,10 +204,7 @@
         pick = jnp.concatenate([onehot, onehot, onehot], axis=1).astype(BF16)
         for q in range(4):
             c = ctf[:, pl.ds(pl.multiple_of((18 * q + base) * 128, 128), 1152)]
-            hi = c.astype(BF16).astype(F32)
-            mid = (c - hi).astype(BF16).astype(F32)
-            low = c - hi - mid
-            parts = jnp.concatenate([hi, mid, low], axis=0).astype(BF16)
+            parts = three_parts(c)
             crow[:, q * 1152:(q + 1) * 1152] = jnp.dot(pick, parts, preferred_element_type=F32)
 
         def widen(n, carry):
@@ -201,7 +243,7 @@
                     for j, (dst, half) in enumerate(((shifted, 0), (shifted, 1), (back, 0), (back, 1))):
                         wide = pl.ds(pl.multiple_of(tt * 256 + half * 128, 128), 128)
                         both = jnp.concatenate([pairs[0][j], pairs[1][j]], axis=0).astype(BF16)
-                        dst[who, pl.ds(8 * (k - 1), 16), wide] = both
+                        dst[pl.ds(pl.multiple_of(who * ROWS + 8 * (k - 1), 16), 16), wide] = both
                     pairs = []
         return carry
 
@@ -250,15 +292,14 @@
 
     lax.fori_loop(0, 12, table, (start_c, start_s))
 
-    copies[5].wait()
     copies[6].wait()
     prepare(core)
 
     other = (x * 2 + 1 - yh) * 2
 
     def hand_on(chunk):
-        first, count = LIB_CHUNKS[chunk]
-        rows = pl.ds(first * 4, count * 4)
+        first, count, length = LIB_CHUNKS[chunk]
+        rows = pl.ds(first * 4, length)
         for k in range(2):
             arrival(lib_in.at[other + k, rows], far_slots[chunk][k]).wait_recv()
         slots = []
@@ -283,11 +324,10 @@
     hand_on(2)
     lax.fori_loop(6, 12, functools.partial(shift_tiles, mate), 0, unroll=2)
 
-    powers = jnp.zeros((CLASSES, POSES), F32)
-    total = [jnp.zeros((ROWS, POSES), F32)] * 2
+    total = jnp.zeros((2 * ROWS, POSES), F32)
     arrival(lib_in.at[0], 1).wait_recv()
-    for chunk, (first, count) in enumerate(LIB_CHUNKS):
-        rows = pl.ds(first * 4, count * 4)
+    for chunk, (first, count, length) in enumerate(LIB_CHUNKS):
+        rows = pl.ds(first * 4, length)
         for pick in first_slots[3 * chunk:3 * chunk + 3]:
             for slot in pick:
                 arrival(lib_in.at[0, rows], slot).wait_recv()
@@ -295,7 +335,8 @@
             copy.wait_recv()
 
         def widen_lib(k, carry):
-            lib_f[pl.ds(pl.multiple_of(k * BLOCK + first * 4, 16), count * 4), :] = lib_in[k, rows, :].astype(F32)
+            tiles = pl.ds(first * 4, count * 4)
+            lib_f[pl.ds(pl.multiple_of(k * BLOCK + first * 4, 16), count * 4), :] = lib_in[k, tiles, :].astype(F32)
             return carry
 
         lax.fori_loop(0, 16, widen_lib, 0)
@@ -312,31 +353,25 @@
                     halves.append(jnp.concatenate(parts, axis=0))
                 cols = pl.ds(pl.multiple_of(tt * 256, 256), 256)
                 lib_b[:, cols] = jnp.concatenate(halves, axis=1).astype(BF16)
-                cols = pl.ds(pl.multiple_of(tt * 128, 128), 128)
-                power_f[:, cols] = halves[0] * halves[0] + halves[1] * halves[1]
             return carry
 
         lax.fori_loop(0, count // 4, gather_tiles, 0)
-        for q in range(4):
-            lo, hi = max(first, 9 * q), min(first + count, 9 * q + 9)
-            if lo < hi:
-                c = ctf[:, pl.ds(pl.multiple_of((9 * q + base + lo) * 128, 128), (hi - lo) * 128)]
-                powers = powers + lax.dot_general(
-                    c * c, power_f[:, lo * 128:hi * 128], (((1,), (1,)), ((), ())),
-                    precision=lax.Precision.HIGHEST, preferred_element_type=F32,
-                )
         cols = slice(first * 256, (first + count) * 256)
-        for c in range(2):
-            total[c] = total[c] + lax.dot_general(
-                shifted[c, :, cols], lib_b[:, cols], (((1,), (1,)), ((), ())), preferred_element_type=F32
-            )
+        total = total + lax.dot_general(
+            shifted[:, cols], lib_b[:, cols], (((1,), (1,)), ((), ())), preferred_element_type=F32
+        )
+    powers = jnp.zeros((8, 128), F32)
+    for k in range(16):
+        powers = powers + lib_in[k, pl.ds(BLOCK, 16), :].astype(F32)[0:8, :]
+    powers = powers[:, 0:32] + powers[:, 32:64] + powers[:, 64:96]
     klass = [meta[c][:, 0:1] for c in range(2)]
-    parts = []
+    parts, bias = [], []
     for c in range(2):
         class_power = jnp.zeros((CAP, POSES), F32)
         for k in range(CLASSES):
             class_power = class_power + jnp.where(klass[c] == float(k), powers[k:k + 1, :], 0.0)
-        parts.append([total[c][s * CAP:(s + 1) * CAP, :] - 0.5 * class_power for s in range(SHIFTS)])
+        bias.append(0.5 * class_power)
+        parts.append([total[c * ROWS + s * CAP:c * ROWS + (s + 1) * CAP, :] for s in range(SHIFTS)])
         for s in range(SHIFTS):
             mine[c, s * CAP:(s + 1) * CAP, 0:POSES] = parts[c][s]
     score_copy = remote(mine, theirs, pair)
@@ -346,7 +381,7 @@
     log_norm, weights = [], []
     for c in range(2):
         prec, live = meta[c][:, 1:2], meta[c][:, 2:3] > 0.5
-        scores = [prec * (parts[c][s] + theirs[c, s * CAP:(s + 1) * CAP, 0:POSES]) for s in range(SHIFTS)]
+        scores = [prec * (parts[c][s] + theirs[c, s * CAP:(s + 1) * CAP, 0:POSES] - bias[c]) for s in range(SHIFTS)]
         top = scores[0]
         for s in range(1, SHIFTS):
             top = jnp.maximum(top, scores[s])
@@ -363,14 +398,10 @@
         unit.astype(F32).astype(BF16), weight, (((1,), (1,)), ((), ())), preferred_element_type=F32
     ).astype(BF16)
 
-    x_sends = []
-    for first, count in CHUNKS:
-        rows = pl.ds(64 * first, 64 * count)
-
+    def sum_tiles(first, count):
         def sum_quarter(q, carry):
             cols = pl.ds(pl.multiple_of((q * 9 + first) * 256, 256), count * 256)
-            part = jnp.dot(weight_t[:, 0:ROWS], back[0, :, cols], preferred_element_type=F32)
-            part = part + jnp.dot(weight_t[:, ROWS:2 * ROWS], back[1, :, cols], preferred_element_type=F32)
+            part = jnp.dot(weight_t, back[:, cols], preferred_element_type=F32)
             for c in range(2):
                 for p in range(2):
                     r = c * 16 + p * 8
@@ -380,6 +411,25 @@
             return carry
 
         lax.fori_loop(0, 4, sum_quarter, 0)
+
+    sum_tiles(0, LEAD)
+    lead_rows = 8 * LEAD
+    for g in range(8):
+        for px in range(4):
+            rows = pl.ds(px * lead_rows, lead_rows)
+            lead_out[g, rows, :] = acc[(px * 8 + g) * lead_rows:(px * 8 + g + 1) * lead_rows, :].astype(BF16)
+    lead_sends = []
+    for d in (4, 3, 5, 2, 6, 1, 7):
+        py = (y + d) % 8
+        copy = remote(lead_out.at[py], lead_in.at[d - 1], device(x, py, z, core))
+        copy.start()
+        lead_sends.append(copy)
+    sent += lead_sends
+
+    x_sends = []
+    for first, count in CHUNKS:
+        rows = pl.ds(64 * first, 64 * count)
+        sum_tiles(first, count)
         chunk_sends = []
         for d in (2, 1, 3):
             at = pl.multiple_of(256 * first + (x + d) % 4 * 64 * count, 64)
@@ -402,7 +452,7 @@
         part = acc[pl.ds(pl.multiple_of(256 * first + x * 64 * count, 64), 64 * count), :]
         for d in range(3):
             part = part + x_in[d, rows, :].astype(F32)
-        room = pl.ds(8 * first, max(size, 16))
+        room = pl.ds(8 * first, 16)
         for g in range(8):
             piece = part[g * size:(g + 1) * size, :]
             y_own[g, pl.ds(8 * first, size), :] = piece
@@ -417,14 +467,40 @@
             chunk_sends.append(copy)
         y_sends.append(chunk_sends)
         sent += chunk_sends
+    for copy in lead_sends:
+        copy.wait_recv()
+    part = jnp.concatenate(
+        [acc[pl.ds(pl.multiple_of((px * 8 + y) * lead_rows, 16), lead_rows), :] for px in range(4)], axis=0
+    )
+    for d in range(7):
+        part = part + lead_in[d].astype(F32)
+    for px in range(4):
+        piece = part[px * lead_rows:(px + 1) * lead_rows, :]
+        last_own[px] = piece
+        last_out[px] = piece.astype(BF16)
+    last_sends = []
+    for d in (2, 1, 3):
+        px = (x + d) % 4
+        copy = remote(last_out.at[px], last_in.at[d - 1], device(px, y, z, core))
+        copy.start()
+        last_sends.append(copy)
+    sent += last_sends
+
     for (first, count), chunk_sends in zip(CHUNKS, y_sends):
         size = 8 * count
         for copy in chunk_sends:
             copy.wait_recv()
         part = y_own[y, pl.ds(8 * first, size), :]
         for d in range(7):
-            part = part + y_in[d, pl.ds(8 * first, max(size, 16)), :].astype(F32)[0:size, :]
+            part = part + y_in[d, pl.ds(8 * first, 16), :].astype(F32)[0:size, :]
         z_own[pl.ds(8 * first, size), :] = part
+
+    for copy in last_sends:
+        copy.wait_recv()
+    part = last_own[x]
+    for d in range(3):
+        part = part + last_in[d].astype(F32)
+    z_own[0:lead_rows, :] = part
 
     zeros4 = jnp.zeros((4, 128), F32)
     for k in range(4):
@@ -513,16 +589,16 @@
             pltpu.VMEM((CAP * RAW, 128), F32),
             pltpu.VMEM((CAP, HALF // 2), F32),
             pltpu.VMEM((2, 16, HALF // 2), F32),
-            pltpu.VMEM((2, ROWS, HALF), BF16),
-            pltpu.VMEM((2, ROWS, HALF), BF16),
+            pltpu.VMEM((2 * ROWS, HALF), BF16),
+            pltpu.VMEM((2 * ROWS, HALF), BF16),
             pltpu.VMEM((2, CAP, 128), F32),
             pltpu.VMEM((2 * RAW, 128), F32),
             pltpu.VMEM((2 * BLOCK, 128), F32),
-            pltpu.VMEM((2, BLOCK, 128), BF16),
-            pltpu.VMEM((16, BLOCK, 128), BF16),
+            pltpu.VMEM((2, TILES, 128), F32),
+            pltpu.VMEM((2, FULL, 128), BF16),
+            pltpu.VMEM((16, FULL, 128), BF16),
             pltpu.VMEM((16 * BLOCK, 128), F32),
             pltpu.VMEM((POSES, HALF), BF16),
-            pltpu.VMEM((POSES, HALF // 2), F32),
             pltpu.VMEM((2, ROWS, 128), F32),
             pltpu.VMEM((2, ROWS, 128), F32),
             pltpu.VMEM((32 * 72, 128), F32),
@@ -531,6 +607,11 @@
             pltpu.VMEM((8, 72, 128), F32),
             pltpu.VMEM((8, 80, 128), BF16),
             pltpu.VMEM((7, 80, 128), BF16),
+            pltpu.VMEM((8, 32 * LEAD, 128), BF16),
+            pltpu.VMEM((7, 32 * LEAD, 128), BF16),
+            pltpu.VMEM((4, 8 * LEAD, 128), F32),
+            pltpu.VMEM((4, 8 * LEAD, 128), BF16),
+            pltpu.VMEM((3, 8 * LEAD, 128), BF16),
             pltpu.VMEM((72, 128), F32),
             pltpu.VMEM((8, 16, 128), F32),
             pltpu.VMEM((8, 16, 128), BF16),

time: 54.5 us -> 54.5 us (level)
  no operation moved by 1% of the time
where the time goes in v4:
time: 54.5 us; the launch traced here: 54.3 us
  Pallas kernels  51.2 us (94%)
  local copies, waits for them, and re-layouts  1.78 us (3%)
  between operations  1.29 us (2%)
    pallas_call x1, Pallas kernels, body(): pl.pallas_call(kernel, out_shape=(jax.ShapeDtypeStruct((2, 2, 384), F32),...  51.2 us
    slice x1, local copies, waits for them, and re-layouts, body(): return (accum[:, :, :HALF // 32], norm.reshape(128)[:CAP])  1.18 us

profile of v4, /device:TPU:1, one launch (start us, length us, event | category | flops | bytes accessed | tf_op | source)
XLA Modules:
  0.0 54.3 jit_solution(4282711211129607384)
XLA Ops:
  1.3 51.2 %expectation.1 = (f32[2,2,384]{2,1,0:T(2,128)}, f32[1,128]{1,0:T(1,128)}) custom-call(s32[1,24]{1,0:T(1,128)} %bitcast.22, f32[1,24]{1,0:T(1,128)} %bitcast.23, s32[1,1]{1,0:T(1,128)} %bitcast.17.counts_hbm, s32[2,9]{1,0:T(2,128)} %bitcast.21, bf16[3456,128]{1,0:T(8,128)(2,1)} %bitcast.18, f32[8,9216]{1,0:T(8,128)} %ctf_hbm.1, bf16[288,128]{1,0:T(8,128)(2,1)} %bitcast.19), custom_call_target="tpu_custom_call" | custom-call | tf_op jit(solution)/shard_map/expectation/pallas_call | solution.py:573
  52.5 0.0 copy-start
  52.5 1.2 %slice_bitcast_fusion = f32[24]{0:T(128)} fusion(f32[1,128]{1,0:T(1,128)} %get-tuple-element.5), kind=kLoop, calls=%fused_computation | loop fusion | bytes 192 | tf_op jit(solution)/shard_map/slice | solution.py:631
  53.7 0.0 copy-done
  53.7 0.6 %copy.13 = f32[2,2,288]{2,1,0:T(2,128)} copy(f32[2,2,288]{2,1,0:T(2,128)S(1)} %bitcast.20) | data formatting | bytes 9216
Async XLA Ops:
  52.5 1.2 %copy-start = (f32[2,2,384]{2,1,0:T(2,128)S(1)}, f32[2,2,384]{2,1,0:T(2,128)}, u32[]{:S(2)}) copy-start(f32[2,2,384]{2,1,0:T(2,128)} %get-tuple-element.4) | copy-start | bytes 18436
